TPU v7x, 32 devices: a whole 2x2x4 slice. The times are simulated.
32 devices in a mesh: replica: 4 (over y, x), fsdp: 8 (over z, core).
Axes of the slice: x: 2, y: 2, z: 4, core: 2. Of those that a mesh axis runs over, the one named last changes fastest.
Arguments:
- tokens: bfloat16 [32768, 1280], P(('replica', 'fsdp')), may hold values from -6 to 6
- lengths: int32 [32], P(('replica', 'fsdp')), may hold values from 256 to 1024, as said below
- cotangent: bfloat16 [32768, 1280], P(('replica', 'fsdp')), may hold values from -6 to 6
- query_weight: bfloat16 [1280, 1280], P('fsdp'), may hold values from -0.15625 to 0.15625
- key_weight: bfloat16 [1280, 1280], P('fsdp'), may hold values from -0.15625 to 0.15625
- value_weight: bfloat16 [1280, 1280], P('fsdp'), may hold values from -0.15625 to 0.15625
- output_weight: bfloat16 [1280, 1280], P('fsdp'), may hold values from -1.25 to 1.25
- up_weight: bfloat16 [1280, 1280], P('fsdp'), may hold values from -0.15625 to 0.15625
- down_weight: bfloat16 [1280, 1280], P('fsdp'), may hold values from -0.15625 to 0.15625
- attn_gain: bfloat16 [1280], P('fsdp'), may hold values from 0.099609375 to 1.8984375
- mlp_gain: bfloat16 [1280], P('fsdp'), may hold values from 0.099609375 to 1.8984375
- up_bias: bfloat16 [1280], P('fsdp'), may hold values from -3 to 3
- down_bias: bfloat16 [1280], P('fsdp'), may hold values from -1.796875 to 1.796875
- query_scale: bfloat16 [80], replicated, may hold values from 0.5 to 2
Outputs:
- output: bfloat16 [32768, 1280], P(('replica', 'fsdp'))
- input_grad: bfloat16 [32768, 1280], P(('replica', 'fsdp'))
- query_grad: float32 [1280, 1280], P('fsdp')
- key_grad: float32 [1280, 1280], P('fsdp')
- value_grad: float32 [1280, 1280], P('fsdp')
- output_grad: float32 [1280, 1280], P('fsdp')
- up_grad: float32 [1280, 1280], P('fsdp')
- down_grad: float32 [1280, 1280], P('fsdp')
- attn_gain_grad: float32 [1280], P('fsdp')
- mlp_gain_grad: float32 [1280], P('fsdp')
- up_bias_grad: float32 [1280], P('fsdp')
- down_bias_grad: float32 [1280], P('fsdp')
- scale_grad: float32 [80], replicated
Inputs may be any that keep to these rules, and one draw needn't show every extreme that they name: `lengths`: valid tokens of each slot; some slot has exactly 1024 and some exactly 256.
All inputs are finite; a program needn't handle non-finite values.
Results may differ from a plain program's by a relative error of at most 0.017.
Values may be sent and summed in bfloat16 or wider, within the bound.
No kernel may reach another device: no remote copies, remote signals or barrier semaphores. Data moves between devices by JAX's collectives and lax.ppermute only.
A program may use at most 384 MiB of HBM per device.

v0:
```python
import jax
import jax.numpy as jnp
from jax import lax
from jax.sharding import PartitionSpec as P

D = 1280
HEADS = 16
HD = 80
FF = 1280
SEQ = 1024


EPS = 1e-06


def rms_parts(v):
    inverse = lax.rsqrt(jnp.mean(v * v, axis=-1, keepdims=True) + EPS)
    return (v * inverse, inverse)


def rms_back(grad_n, normed, inverse):
    return inverse * (grad_n - normed * jnp.mean(grad_n * normed, axis=-1, keepdims=True))


def outer_sum(left, right):
    return lax.dot_general(
        left, right, (((0,), (0,)), ((), ())), preferred_element_type=jnp.float32
    )


def back_mul(grad, weight):
    return lax.dot_general(
        grad, weight, (((1,), (1,)), ((), ())), preferred_element_type=jnp.float32
    )


def slot_probs(scaled, keys, length):
    positions = jnp.arange(SEQ, dtype=jnp.int32)
    allowed = (positions[None, :] <= positions[:, None]) & (positions[None, :] < length)
    scores = jnp.einsum(
        "qhd,khd->hqk",
        scaled.reshape(SEQ, HEADS, HD),
        keys.reshape(SEQ, HEADS, HD),
        preferred_element_type=jnp.float32,
    )
    return jnp.where(allowed[None], scores, -1e30)


def slot_forward(pack):
    scaled, keys, values, length = pack
    masked = slot_probs(scaled, keys, length)
    top = jnp.max(masked, axis=-1, keepdims=True)
    logsum = top + jnp.log(jnp.sum(jnp.exp(masked - top), axis=-1, keepdims=True))
    probs_low = jnp.exp(masked - logsum).astype(jnp.bfloat16)
    attended = jnp.einsum(
        "hqk,khd->qhd",
        probs_low,
        values.reshape(SEQ, HEADS, HD),
        preferred_element_type=jnp.float32,
    )
    return (attended.reshape(SEQ, D), logsum)


def slot_backward(pack):
    scaled, keys, values, length, logsum, grad_att = pack
    probs = jnp.exp(slot_probs(scaled, keys, length) - logsum)
    probs_low = probs.astype(jnp.bfloat16)
    grad_r = grad_att.reshape(SEQ, HEADS, HD)
    grad_probs = jnp.einsum(
        "qhd,khd->hqk", grad_r, values.reshape(SEQ, HEADS, HD), preferred_element_type=jnp.float32
    )
    value_part = jnp.einsum("hqk,qhd->khd", probs_low, grad_r, preferred_element_type=jnp.float32)
    grad_scores = (
        probs * (grad_probs - jnp.sum(probs * grad_probs, axis=-1, keepdims=True))
    ).astype(jnp.bfloat16)
    grad_scaled = jnp.einsum(
        "hqk,khd->qhd",
        grad_scores,
        keys.reshape(SEQ, HEADS, HD),
        preferred_element_type=jnp.float32,
    )
    grad_keys = jnp.einsum(
        "hqk,qhd->khd",
        grad_scores,
        scaled.reshape(SEQ, HEADS, HD),
        preferred_element_type=jnp.float32,
    )
    return (grad_scaled.reshape(SEQ, D), grad_keys.reshape(SEQ, D), value_part.reshape(SEQ, D))


def shards(
    tokens,
    lengths,
    cotangent,
    query_weight,
    key_weight,
    value_weight,
    output_weight,
    up_weight,
    down_weight,
    attn_gain,
    mlp_gain,
    up_bias,
    down_bias,
    query_scale,
):
    wq, wk, wv, wo, w_up, w_down, gain_a, gain_m, bias_up, bias_down = (
        lax.all_gather(query_weight, "fsdp", axis=0, tiled=True),
        lax.all_gather(key_weight, "fsdp", axis=0, tiled=True),
        lax.all_gather(value_weight, "fsdp", axis=0, tiled=True),
        lax.all_gather(output_weight, "fsdp", axis=0, tiled=True),
        lax.all_gather(up_weight, "fsdp", axis=0, tiled=True),
        lax.all_gather(down_weight, "fsdp", axis=0, tiled=True),
        lax.all_gather(attn_gain, "fsdp", axis=0, tiled=True),
        lax.all_gather(mlp_gain, "fsdp", axis=0, tiled=True),
        lax.all_gather(up_bias, "fsdp", axis=0, tiled=True),
        lax.all_gather(down_bias, "fsdp", axis=0, tiled=True),
    )
    slots = lengths.shape[0]
    xin = tokens.astype(jnp.float32)
    normed1, inverse1 = rms_parts(xin)
    attn_in = (normed1 * gain_a.astype(jnp.float32)).astype(jnp.bfloat16)
    query_raw = jnp.dot(attn_in, wq, preferred_element_type=jnp.float32)
    factor = query_scale.astype(jnp.float32) * (1.0 / jnp.sqrt(jnp.float32(HD)))
    scale_row = jnp.tile(factor, HEADS)
    scaled = (query_raw * scale_row).astype(jnp.bfloat16)
    keys = jnp.dot(attn_in, wk, preferred_element_type=jnp.float32).astype(jnp.bfloat16)
    values = jnp.dot(attn_in, wv, preferred_element_type=jnp.float32).astype(jnp.bfloat16)
    scaled3 = scaled.reshape(slots, SEQ, D)
    keys3 = keys.reshape(slots, SEQ, D)
    values3 = values.reshape(slots, SEQ, D)
    attended, logsums = lax.map(slot_forward, (scaled3, keys3, values3, lengths))
    attended = attended.reshape(-1, D).astype(jnp.bfloat16)
    hidden1 = xin + jnp.dot(attended, wo, preferred_element_type=jnp.float32)
    normed2, inverse2 = rms_parts(hidden1)
    mlp_in = (normed2 * gain_m.astype(jnp.float32)).astype(jnp.bfloat16)
    pre = jnp.dot(mlp_in, w_up, preferred_element_type=jnp.float32) + bias_up.astype(jnp.float32)
    act = jax.nn.silu(pre).astype(jnp.bfloat16)
    out_f = (
        hidden1
        + jnp.dot(act, w_down, preferred_element_type=jnp.float32)
        + bias_down.astype(jnp.float32)
    )
    wq, wk, wv, wo, w_up, w_down, gain_a, gain_m = (
        lax.all_gather(query_weight, "fsdp", axis=0, tiled=True),
        lax.all_gather(key_weight, "fsdp", axis=0, tiled=True),
        lax.all_gather(value_weight, "fsdp", axis=0, tiled=True),
        lax.all_gather(output_weight, "fsdp", axis=0, tiled=True),
        lax.all_gather(up_weight, "fsdp", axis=0, tiled=True),
        lax.all_gather(down_weight, "fsdp", axis=0, tiled=True),
        lax.all_gather(attn_gain, "fsdp", axis=0, tiled=True),
        lax.all_gather(mlp_gain, "fsdp", axis=0, tiled=True),
    )
    positions = jnp.arange(SEQ, dtype=jnp.int32)
    valid = (positions[None, :] < lengths[:, None]).reshape(-1, 1).astype(jnp.float32)
    grad_out = cotangent.astype(jnp.float32) * valid
    grad_out_low = grad_out.astype(jnp.bfloat16)
    down_bias_grad = jnp.sum(grad_out_low.astype(jnp.float32), axis=0)
    sigma = jax.nn.sigmoid(pre)
    grad_pre = (back_mul(grad_out_low, w_down) * (sigma * (1.0 + pre * (1.0 - sigma)))).astype(
        jnp.bfloat16
    )
    up_bias_grad = jnp.sum(grad_pre.astype(jnp.float32), axis=0)
    grad_mlp_in = back_mul(grad_pre, w_up)
    mlp_gain_grad = jnp.sum(grad_mlp_in * normed2, axis=0)
    grad_hidden = grad_out + rms_back(grad_mlp_in * gain_m.astype(jnp.float32), normed2, inverse2)
    grad_proj = grad_hidden.astype(jnp.bfloat16)
    grad_att = back_mul(grad_proj, wo).astype(jnp.bfloat16)
    grad_scaled, grad_keys, grad_values = lax.map(
        slot_backward, (scaled3, keys3, values3, lengths, logsums, grad_att.reshape(slots, SEQ, D))
    )
    grad_scaled = grad_scaled.reshape(-1, D).astype(jnp.bfloat16)
    grad_keys = grad_keys.reshape(-1, D).astype(jnp.bfloat16)
    grad_values = grad_values.reshape(-1, D).astype(jnp.bfloat16)
    scaled_f = grad_scaled.astype(jnp.float32)
    scale_part = jnp.sum((scaled_f * query_raw).reshape(-1, HEADS, HD), axis=(0, 1)) * (
        1.0 / jnp.sqrt(jnp.float32(HD))
    )
    grad_query = (scaled_f * scale_row).astype(jnp.bfloat16)
    grad_attn_in = back_mul(grad_query, wq) + back_mul(grad_keys, wk) + back_mul(grad_values, wv)
    attn_gain_grad = jnp.sum(grad_attn_in * normed1, axis=0)
    input_grad = grad_hidden + rms_back(
        grad_attn_in * gain_a.astype(jnp.float32), normed1, inverse1
    )

    def rows_of(left, grad):
        return outer_sum(left, grad)

    owned = lax.psum_scatter(
        jnp.concatenate(
            [
                rows_of(attn_in, grad_query),
                rows_of(attn_in, grad_keys),
                rows_of(attn_in, grad_values),
                rows_of(attended, grad_proj),
                rows_of(mlp_in, grad_pre),
                rows_of(act, grad_out_low),
            ],
            axis=1,
        ),
        "fsdp",
        scatter_dimension=0,
        tiled=True,
    )
    vectors = (
        lax.psum_scatter(attn_gain_grad, "fsdp", scatter_dimension=0, tiled=True),
        lax.psum_scatter(mlp_gain_grad, "fsdp", scatter_dimension=0, tiled=True),
        lax.psum_scatter(up_bias_grad, "fsdp", scatter_dimension=0, tiled=True),
        lax.psum_scatter(down_bias_grad, "fsdp", scatter_dimension=0, tiled=True),
    )
    summed = (
        lax.psum(owned.astype(jnp.bfloat16), "replica").astype(jnp.float32),
        lax.psum(vectors[0].astype(jnp.bfloat16), "replica").astype(jnp.float32),
        lax.psum(vectors[1].astype(jnp.bfloat16), "replica").astype(jnp.float32),
        lax.psum(vectors[2].astype(jnp.bfloat16), "replica").astype(jnp.float32),
        lax.psum(vectors[3].astype(jnp.bfloat16), "replica").astype(jnp.float32),
    )
    block = summed[0]
    scale_grad = lax.psum(scale_part, ("replica", "fsdp"))
    return (
        out_f.astype(jnp.bfloat16),
        input_grad.astype(jnp.bfloat16),
        block[:, 0:D],
        block[:, D : 2 * D],
        block[:, 2 * D : 3 * D],
        block[:, 3 * D : 4 * D],
        block[:, 4 * D : 4 * D + FF],
        block[:, 4 * D + FF : 5 * D + FF],
        summed[1],
        summed[2],
        summed[3],
        summed[4],
        scale_grad,
    )


def solution(mesh):
    placed = (
        P(("replica", "fsdp"), None),
        P(("replica", "fsdp")),
        P(("replica", "fsdp"), None),
        P("fsdp", None),
        P("fsdp", None),
        P("fsdp", None),
        P("fsdp", None),
        P("fsdp", None),
        P("fsdp", None),
        P("fsdp"),
        P("fsdp"),
        P("fsdp"),
        P("fsdp"),
        P(),
    )
    return jax.shard_map(
        shards,
        mesh=mesh,
        in_specs=placed,
        out_specs=(
            P(("replica", "fsdp"), None),
            P(("replica", "fsdp"), None),
            P("fsdp", None),
            P("fsdp", None),
            P("fsdp", None),
            P("fsdp", None),
            P("fsdp", None),
            P("fsdp", None),
            P("fsdp"),
            P("fsdp"),
            P("fsdp"),
            P("fsdp"),
            P(),
        ),
        check_vma=False,
    )
```

profile of v0, /device:TPU:0, one launch (start us, length us, event | category | flops | bytes accessed | tf_op | source)
XLA Modules:
  0.0 1037.8 jit_solution(6463155360054573920)
XLA Ops:
  7.2 0.7 all-gather.11.cloned.1.call-update
  8.0 0.7 all-gather.9.cloned.1.call-update
  8.7 0.7 all-gather.7.cloned.1.call-update
  11.8 0.7 convert_multiply_fusion.3
  12.5 2.3 fusion.12
  14.9 1.3 fusion.42
  16.9 0.9 dynamic-update-slice.2
  17.7 0.8 dynamic-update-slice.1
  18.6 0.8 dynamic-update-slice
  19.4 0.8 dynamic-update-slice.3
  20.3 31.9 %all-reduce.9 = (bf16[1280]{0:T(1024)(128)(2,1)S(1)}, bf16[1280]{0:T(1024)(128)(2,1)S(1)}, bf16[1280]{0:T(1024)(128)(2,1)S(1)}, bf16[1280]{0:T(1024)(128)(2,1)}) all-reduce(bf16[1280]{0:T(1024)(128)(2,1)S(1)} %dynamic-update-slice, bf16[1280]{0:T(1024)(128)(2,1)S(1)} %dynamic-update-slice.1, ...), channel_id=1, replica_groups=mesh['replica'=4,'fsdp'=8] {'fsdp'}, use_global_device_ids=true, to_apply=%add | all-reduce | flops 5120 | bytes 20480
  52.7 7.8 convolution_convert_fusion.1
  60.5 4.7 copy.80
  65.2 27.0 %all-gather.9.cloned.1.call-done = bf16[1280,1280]{1,0:T(8,128)(2,1)} async-done(((bf16[160,1280]{1,0:T(8,128)(2,1)}), bf16[1280,1280]{1,0:T(8,128)(2,1)}) %all-gather.9.cloned.1.call-update) | async-done | bytes 3276816 | tf_op jit(solution)/shard_map/all_gather | solution.py:108
  92.2 9.5 multiply_convert_fusion.5
  101.8 4.4 copy.79
  106.2 26.1 %select_reduce_fusion = (f32[16,1024]{1,0:T(8,128)S(1)}, f32[16,1024,1024]{1,2,0:T(8,128)}) fusion(pred[1024,1024]{0,1:T(8,128)(4,1)S(1)} %fusion.18, bf16[1024,16,80]{0,2,1:T(8,128)(2,1)} %bitcast.52, bf16[1024,16,80]{0,2,1:T(8,128)(2,1)} %bitcast.54), kind=kOutput, calls=%fused_computation.4 | convolution fusion | flops 2717892608 | bytes 73465856 | tf_op jit(solution)/shard_map/while/body/eval_jaxpr/qhd,khd->hqk/dot_general | solution.py:40
  132.3 22.2 %exponential_reduce_fusion = f32[16,1024]{1,0:T(8,128)S(1)} fusion(f32[16,1024,1024]{1,2,0:T(8,128)} %get-tuple-element.145, f32[16,1024]{1,0:T(8,128)S(1)} %get-tuple-element.144, pred[1024,1024]{0,1:T(8,128)(4,1)S(1)} %fusion.18), kind=kLoop, calls=%fused_computation.3 | loop fusion | flops 50315264 | bytes 68288512 | tf_op jit(solution)/shard_map/while/body/eval_jaxpr/reduce_sum | solution.py:53
  154.6 7.9 convolution_convert_fusion.2
  162.5 4.4 copy.78
  166.9 27.0 %fusion.19 = bf16[16,80,1024]{2,1,0:T(8,128)(2,1)} fusion(bf16[1024,16,80]{0,2,1:T(8,128)(2,1)} %bitcast.61, f32[16,1024,1024]{1,2,0:T(8,128)} %get-tuple-element.145, f32[16,1024]{1,0:T(8,128)S(1)} %log_add_fusion, pred[1024,1024]{0,1:T(8,128)(4,1)S(1)} %fusion.18), kind=kOutput, calls=%fused_computation.52 | convolution fusion | flops 2735996928 | bytes 73465856 | tf_op jit(solution)/shard_map/while/body/eval_jaxpr/hqk,khd->qhd/dot_general | solution.py:55
  193.9 9.7 multiply_reduce_fusion.4
  203.7 8.0 all-gather.15.cloned.1.call-done
  211.6 9.4 fusion.33
  221.0 30.4 %all-gather.17.cloned.1.call-done = bf16[1280,1280]{1,0:T(8,128)(2,1)} async-done(((bf16[160,1280]{1,0:T(8,128)(2,1)}), bf16[1280,1280]{1,0:T(8,128)(2,1)}) %all-gather.17.cloned.1.call-update) | async-done | bytes 3276816 | tf_op jit(solution)/shard_map/all_gather | solution.py:113
  251.4 9.5 convert_reduce_fusion.1
  260.9 4.6 multiply_reduce_fusion.2
  265.6 2.7 convert_reduce_fusion
  268.2 2.3 copy-done.3
  270.6 4.9 convolution_convert_fusion
  275.5 4.5 copy.82
  280.0 26.1 %fusion.22 = bf16[16,80,1024]{2,1,0:T(8,128)(2,1)} fusion(bf16[1024,16,80]{0,2,1:T(8,128)(2,1)} %bitcast.63, f32[16,1024,1024]{1,2,0:T(8,128)} %get-tuple-element.145, f32[16,1024]{1,0:T(8,128)S(1)} %log_add_fusion, pred[1024,1024]{0,1:T(8,128)(4,1)S(1)} %fusion.18), kind=kOutput, calls=%fused_computation.53 | convolution fusion | flops 2735996928 | bytes 73465856 | tf_op jit(solution)/shard_map/while/body/eval_jaxpr/hqk,qhd->khd/dot_general | solution.py:72
  306.1 49.2 %multiply_reduce_fusion = (f32[16,1024]{1,0:T(8,128)S(1)}, f32[16,1024,1024]{1,2,0:T(8,128)}) fusion(f32[16,1024,1024]{1,2,0:T(8,128)} %get-tuple-element.145, f32[16,1024]{1,0:T(8,128)S(1)} %log_add_fusion, pred[1024,1024]{0,1:T(8,128)(4,1)S(1)} %fusion.18, bf16[1024,16,80]{0,2,1:T(8,128)(2,1)} %bitcast.64, bf16[1024,16,80]{0,2,1:T(8,128)(2,1)} %bitcast.62), kind=kOutput, calls=%fused_computation.1 | convolution fusion | flops 2751447040 | bytes 140640256 | tf_op jit(solution)/shard_map/while/body/eval_jaxpr/qhd,khd->hqk/dot_general | solution.py:69
  355.3 53.8 %multiply_convert_fusion = bf16[16,1024,1024]{1,2,0:T(8,128)(2,1)} fusion(f32[16,1024,1024]{1,2,0:T(8,128)} %get-tuple-element.150, f32[16,1024,1024]{1,2,0:T(8,128)} %get-tuple-element.145, f32[16,1024]{1,0:T(8,128)S(1)} %get-tuple-element.149, f32[16,1024]{1,0:T(8,128)S(1)} %log_add_fusion, pred[1024,1024]{0,1:T(8,128)(4,1)S(1)} %fusion.18), kind=kLoop, calls=%fused_computation | loop fusion | flops 83886080 | bytes 168951808 | tf_op jit(solution)/shard_map/while/body/eval_jaxpr/convert_element_type | solution.py:75
  409.2 17.0 %convolution_convert_fusion.3 = bf16[16,80,1024]{2,1,0:T(8,128)(2,1)} fusion(bf16[1024,16,80]{0,2,1:T(8,128)(2,1)} %bitcast.53, bf16[16,1024,1024]{1,2,0:T(8,128)(2,1)} %multiply_convert_fusion), kind=kOutput, calls=%fused_computation.54 | convolution fusion | flops 2685665280 | bytes 38797312 | tf_op jit(solution)/shard_map/while/body/eval_jaxpr/hqk,qhd->khd/dot_general | solution.py:82
  426.2 16.2 %convert_convert_fusion = f32[16,80,1024]{2,1,0:T(8,128)} fusion(bf16[1024,16,80]{0,2,1:T(8,128)(2,1)S(1)} %bitcast.55, bf16[16,1024,1024]{1,2,0:T(8,128)(2,1)} %multiply_convert_fusion), kind=kOutput, calls=%fused_computation.51 | convolution fusion | flops 2686976000 | bytes 41418752 | tf_op jit(solution)/shard_map/while/body/eval_jaxpr/hqk,khd->qhd/dot_general | solution.py:76
  442.4 6.1 copy.84
  448.5 9.0 convolution_dynamic-update-slice_fusion.5
  457.5 5.7 convolution_dynamic-update-slice_fusion.1
  463.2 5.8 convolution_dynamic-update-slice_fusion
  469.1 5.8 convolution_dynamic-update-slice_fusion.4
  474.9 6.5 convolution_dynamic-update-slice_fusion.3
  481.5 6.6 convolution_dynamic-update-slice_fusion.2
  488.1 39.3 %copy.98 = f32[1280,7680]{1,0:T(8,128)} copy(f32[1280,7680]{0,1:T(8,128)} %convolution_dynamic-update-slice_fusion.2) | data formatting | bytes 78643200
  527.5 0.6 copy-done.26
  528.7 5.0 multiply_reduce_fusion.1
  533.8 6.5 fusion.43
  540.3 6.0 fusion.27
  546.4 7.0 fusion.11
  553.3 29.5 %all-reduce.8 = (bf16[1280]{0:T(1024)(128)(2,1)S(1)}, bf16[1280]{0:T(1024)(128)(2,1)S(1)}, bf16[1280]{0:T(1024)(128)(2,1)S(1)}, bf16[1280]{0:T(1024)(128)(2,1)S(1)}) all-reduce(f32[1280]{0:T(1024)S(1)} %get-tuple-element.118, f32[1280]{0:T(1024)S(1)} %copy-done.25, ...), channel_id=3, replica_groups=mesh['replica'=4,'fsdp'=8] {'fsdp'}, use_global_device_ids=true, to_apply=%region_10.11.clone | all-reduce | flops 5120 | bytes 30720
  583.1 9.8 all-reduce.10
  595.2 38.7 %psum.47 = f32[80]{0:T(128)} all-reduce(f32[80]{0:T(128)S(1)} %broadcast_multiply_fusion.2), channel_id=1, replica_groups=mesh['replica'=4,'fsdp'=8] {'replica','fsdp'}, use_global_device_ids=true, to_apply=%region_23.24 | all-reduce | flops 80 | bytes 640 | tf_op jit(solution)/shard_map/psum | solution.py:219
  633.9 273.9 %reduce-scatter.4.cloned.1.call-done = f32[160,7680]{1,0:T(8,128)} async-done(((f32[1280,7680]{1,0:T(8,128)}), f32[160,7680]{1,0:T(8,128)}) %reduce-scatter.4.cloned.1.call-update) | async-done | bytes 4915216
  907.9 6.5 copy.99
  914.4 6.6 fusion.10
  920.9 9.1 add_convert_fusion
  930.1 83.1 %all-reduce.13.cloned.1.call-done = bf16[160,7680]{0,1:T(8,128)(2,1)} async-done(((bf16[160,7680]{0,1:T(8,128)(2,1)}), bf16[160,7680]{0,1:T(8,128)(2,1)}) %all-reduce.13.cloned.1.call-update) | async-done | bytes 2457616 | tf_op jit(solution)/shard_map/psum | solution.py:212
  1013.2 4.7 fusion.41
  1017.9 2.6 copy.93
  1020.5 2.6 copy.92
  1023.1 2.6 copy.91
  1025.7 2.6 copy.90
  1028.3 1.3 copy.89
  1029.6 1.3 copy.88
  (128 shorter events, 5.3 us)
Async XLA Ops:
  7.2 45.5 %all-gather.11.cloned.1.call-start = ((), (), s32[]{:S(2)}) async-start(), calls=%async_computation.3 | async-start | bytes 3686400 | tf_op jit(solution)/shard_map/all_gather | solution.py:109
  7.9 84.3 %all-gather.9.cloned.1.call-start = ((), (), s32[]{:S(2)}) async-start(), calls=%async_computation.2 | async-start | bytes 3686400 | tf_op jit(solution)/shard_map/all_gather | solution.py:108
  8.7 145.9 %all-gather.7.cloned.1.call-start = ((), (), s32[]{:S(2)}) async-start(), calls=%async_computation.1 | async-start | bytes 3686400 | tf_op jit(solution)/shard_map/all_gather | solution.py:110
  9.4 184.5 %all-gather.13.cloned.1.call-start = ((), (), s32[]{:S(2)}) async-start(), calls=%async_computation.4 | async-start | bytes 3686400 | tf_op jit(solution)/shard_map/all_gather | solution.py:111
  10.0 201.6 %all-gather.15.cloned.1.call-start = ((), (), s32[]{:S(2)}) async-start(), calls=%async_computation.5 | async-start | bytes 3686400 | tf_op jit(solution)/shard_map/all_gather | solution.py:112
  10.6 240.8 %all-gather.17.cloned.1.call-start = ((), (), s32[]{:S(2)}) async-start(), calls=%async_computation.6 | async-start | bytes 3686400 | tf_op jit(solution)/shard_map/all_gather | solution.py:113
  11.1 896.7 %reduce-scatter.4.cloned.1.call-start = ((), (), s32[]{:S(2)}) async-start(), calls=%async_computation.8 | async-start | bytes 44236800
  12.5 253.0 %copy-start.16 = (f32[1024]{0:T(1024)}, f32[1024]{0:T(1024)S(1)}, u32[]{:S(2)}) copy-start(f32[1024]{0:T(1024)S(1)} %fusion.28) | copy-start | bytes 12292
  14.9 139.8 %copy-start.14 = (f32[1024]{0:T(1024)}, f32[1024]{0:T(1024)S(1)}, u32[]{:S(2)}) copy-start(f32[1024]{0:T(1024)S(1)} %add_rsqrt_fusion.1) | copy-start | bytes 12292
  52.2 102.4 %copy-start.9 = (f32[1280]{0:T(1024)}, f32[1280]{0:T(1024)S(1)}, u32[]{:S(2)}) copy-start(f32[1280]{0:T(1024)S(1)} %convert_element_type.158) | copy-start | bytes 15364
  52.3 40.0 %copy-start.22 = (f32[1280]{0:T(1024)}, f32[1280]{0:T(1024)S(1)}, u32[]{:S(2)}) copy-start(f32[1280]{0:T(1024)S(1)} %mul.150) | copy-start | bytes 15364
  52.3 213.3 %copy-start.11 = (f32[1280]{0:T(1024)}, f32[1280]{0:T(1024)S(1)}, u32[]{:S(2)}) copy-start(f32[1280]{0:T(1024)S(1)} %convert_element_type.168) | copy-start | bytes 15364
  52.3 199.1 %copy-start.20 = (f32[1280]{0:T(1024)}, f32[1280]{0:T(1024)S(1)}, u32[]{:S(2)}) copy-start(f32[1280]{0:T(1024)S(1)} %convert_element_type.170) | copy-start | bytes 15364
  203.7 61.9 %copy-start.18 = (f32[1024]{0:T(1024)}, f32[1024]{0:T(1024)S(1)}, u32[]{:S(2)}) copy-start(f32[1024]{0:T(1024)S(1)} %add_rsqrt_fusion) | copy-start | bytes 12292
  251.4 9.5 copy-start.2
  251.4 9.5 copy-start.30
  260.9 4.6 copy-start.33
  260.9 4.6 copy-start.7
  265.5 5.0 copy-start.5
  268.2 2.3 copy-start.3
  409.1 17.0 %copy-start = (bf16[1024,1280]{0,1:T(8,128)(2,1)S(1)}, bf16[1024,1280]{0,1:T(8,128)(2,1)}, u32[]{:S(2)}) copy-start(bf16[1024,1280]{0,1:T(8,128)(2,1)} %copy.80) | copy-start | bytes 7864324
  442.4 6.1 copy-start.1
  442.4 6.1 copy-start.10
  442.4 6.1 copy-start.15
  442.4 6.1 copy-start.23
  448.5 9.0 copy-start.4
  457.5 5.7 copy-start.31
  457.5 11.5 %slice-start.2 = ((s8[5242880]{0:T(1024)(128)(4,1)}), s8[4194304]{0:T(1024)(128)(4,1)S(1)}, s32[]{:S(2)}) async-start(s8[5242880]{0:T(1024)(128)(4,1)} %bitcast.59), calls=%async_computation.11 | async-start | bytes 8388608
  457.5 17.3 %slice-start = ((s8[5242880]{0:T(1024)(128)(4,1)}), s8[4194304]{0:T(1024)(128)(4,1)S(1)}, s32[]{:S(2)}) async-start(s8[5242880]{0:T(1024)(128)(4,1)} %bitcast.57), calls=%async_computation.9 | async-start | bytes 8388608
  463.2 5.8 slice-start.3
  463.2 5.8 copy-start.6
  463.2 11.6 %slice-start.1 = ((s8[5242880]{0:T(1024)(128)(4,1)}), s8[1048576]{0:T(1024)(128)(4,1)S(1)}, s32[]{:S(2)}) async-start(s8[5242880]{0:T(1024)(128)(4,1)} %bitcast.57), calls=%async_computation.10 | async-start | bytes 2097152
  469.0 5.8 copy-start.12
  469.0 5.8 copy-start.19
  469.0 5.8 copy-start.34
  469.0 12.4 %slice-start.4 = ((s8[5242880]{0:T(1024)(128)(4,1)}), s8[4194304]{0:T(1024)(128)(4,1)S(1)}, s32[]{:S(2)}) async-start(s8[5242880]{0:T(1024)(128)(4,1)} %bitcast.71), calls=%async_computation.13 | async-start | bytes 8388608
  474.9 6.6 copy-start.8
  474.9 6.6 copy-start.17
  474.9 6.6 copy-start.21
  474.9 6.6 slice-start.5
  527.4 0.7 copy-start.26
  527.4 485.8 %all-reduce.13.cloned.1.call-start = ((), (), s32[]{:S(2)}) async-start(), calls=%async_computation.7 | async-start | bytes 7864320 | tf_op jit(solution)/shard_map/psum | solution.py:212
  533.8 6.5 copy-start.28
  540.3 6.0 copy-start.29
  540.3 6.0 copy-start.32
  546.3 7.0 copy-start.13
  546.3 7.0 copy-start.24
  546.3 7.0 copy-start.25
  914.4 6.6 copy-start.27
Sparse Core Ops, SparseCore 0:
  9.7 42.6 all-gather.10
  54.0 38.1 all-gather.8
  93.9 38.2 all-gather.6
  133.6 38.2 all-gather.12
  173.4 38.2 all-gather.14
  213.1 38.2 all-gather.16
  527.6 380.2 reduce-scatter.3
  914.5 98.6 all-reduce.12
where the time goes:
time: 1050 us; the launch traced here: 1040 us
  waiting for transfers between devices  426 us (41%)
  matrix products  293 us (28%)
  blocking collectives  110 us (10%)
  other arithmetic  96 us (9%)
  local copies, waits for them, and re-layouts  95.8 us (9%)
  between operations  16.8 us (2%)
    unnamed x9, waiting for transfers between devices  278 us
    psum x1, waiting for transfers between devices, shards(): lax.psum(owned.astype(jnp.bfloat16), 'replica').astype(jnp.float32)  83.1 us
    unnamed x103, local copies, waits for them, and re-layouts  66.8 us
    unnamed x2, blocking collectives  61.4 us
    convert_element_type x1, other arithmetic, slot_backward(): grad_scores = (probs * (grad_probs - jnp.sum(probs * grad_probs, axis=-1,...  53.8 us
    dot_general x1, matrix products, slot_backward(): jnp.einsum('qhd,khd->hqk', grad_r, values.reshape(SEQ, HEADS, HD), prefer...  49.2 us
    dot_general x6, matrix products, outer_sum(): lax.dot_general(left, right, (((0,), (0,)), ((), ())), preferred_element_...  39.4 us
    psum x1, blocking collectives, shards(): scale_grad = lax.psum(scale_part, ('replica', 'fsdp'))  38.7 us
  transfers between devices with their start and end apart: 8, of which 5 were waited for; matrix products, arithmetic and copies ran while one was open for 18% of the time, Pallas kernels for 0%

commit v1 on v0

v1 whole, which is shorter than its diff:
```python
import functools
import math

import jax
import jax.numpy as jnp
from jax import lax
from jax.experimental import pallas as pl
from jax.experimental.pallas import tpu as pltpu
from jax.sharding import PartitionSpec as P

D = 1280
HEADS = 16
HD = 80
FF = 1280
SEQ = 1024
EPS = 1e-06
LOG2E = math.log2(math.e)
NEG = -1e30
LANES = 128
BLOCK = 256
GROUP = 8

bf16 = jnp.bfloat16
f32 = jnp.float32


def rms_parts(v):
    inverse = lax.rsqrt(jnp.mean(v * v, axis=-1, keepdims=True) + EPS)
    return (v * inverse, inverse)


def rms_back(grad_n, normed, inverse):
    return inverse * (grad_n - normed * jnp.mean(grad_n * normed, axis=-1, keepdims=True))


def nt(a, b):
    return lax.dot_general(a, b, (((1,), (1,)), ((), ())), preferred_element_type=f32)


def nn(a, b):
    return lax.dot_general(a, b, (((1,), (0,)), ((), ())), preferred_element_type=f32)


def tn(a, b):
    return lax.dot_general(a, b, (((0,), (0,)), ((), ())), preferred_element_type=f32)


def widen(v):
    return jnp.pad(v, ((0, 0), (0, LANES - HD)))


def split3(v):
    a = v.astype(bf16).astype(f32)
    b = (v - a).astype(bf16).astype(f32)
    c = (v - a - b).astype(bf16).astype(f32)
    return a, b, c


def extra_lanes(lane, base, extra):
    out = jnp.zeros_like(base)
    for place, value in reversed(list(enumerate(extra))):
        out = jnp.where(lane == HD + place, value, out)
    return jnp.where(lane < HD, base, out)


def forward_kernel(heads, len_ref, q_ref, k_ref, v_ref, o_ref, qa_ref, ka_ref, va_ref):
    length = len_ref[0]
    lane = lax.broadcasted_iota(jnp.int32, (SEQ, LANES), 1)
    row = lax.broadcasted_iota(jnp.int32, (SEQ, LANES), 0)
    mask = jnp.where(row < length, 0.0, NEG)
    k_pad = jnp.where(lane == HD, mask, jnp.where((lane > HD) & (lane < HD + 4), 1.0, 0.0)).astype(bf16)
    v_pad = jnp.where((lane >= HD) & (lane < HD + 3), 1.0, 0.0).astype(bf16)
    q_pad = jnp.where(lane == HD, 1.0, 0.0).astype(bf16)
    in_head = lane < HD
    block_lane = lane[:BLOCK]
    block_row = lax.broadcasted_iota(jnp.int32, (LANES, BLOCK), 0)
    causal = lax.broadcasted_iota(jnp.int32, (BLOCK, BLOCK), 0) <= lax.broadcasted_iota(
        jnp.int32, (BLOCK, BLOCK), 1
    )
    blocks = SEQ // BLOCK

    def prepare(h):
        own = slice(h * HD, (h + 1) * HD)
        ka_ref[h] = jnp.where(in_head, widen(k_ref[:, own]), k_pad)
        va_ref[h] = jnp.where(in_head, widen(v_ref[:, own]), v_pad)
        qa_ref[h] = jnp.where(in_head, widen(q_ref[:, own]), q_pad)

    def scores(h, i):
        return nt(ka_ref[h, : (i + 1) * BLOCK, :], qa_ref[h, i * BLOCK : (i + 1) * BLOCK, :])

    def attend(h, i, st):
        before = i * BLOCK
        diagonal = jnp.where(causal, st[before:], NEG)
        top = jnp.max(diagonal, axis=0, keepdims=True)
        if i:
            top = jnp.maximum(top, jnp.max(st[:before], axis=0, keepdims=True))
        p = jnp.exp2(diagonal - top).astype(bf16)
        if i:
            p = jnp.concatenate([jnp.exp2(st[:before] - top).astype(bf16), p], axis=0)
        return tn(va_ref[h, : before + BLOCK, :], p), top

    def finish(h, i, ot, top):
        rows = slice(i * BLOCK, (i + 1) * BLOCK)
        total = ot[HD : HD + 1]
        a, b, c = split3(-(top + jnp.log2(total)))
        scaled = jnp.where(block_row < HD, ot / total, 0.0)
        for place, value in ((1, a), (2, b), (3, c)):
            scaled = jnp.where(block_row == HD + place, value, scaled)
        o = scaled.T
        o_ref[rows, h * HD : (h + 1) * HD] = o[:, :HD].astype(bf16)
        qa_ref[h, rows, :] = jnp.where(block_lane <= HD, qa_ref[h, rows, :].astype(f32), o).astype(bf16)

    for h in range(heads):
        prepare(h)
    scored, done = [], []
    for h, i in [(h, i) for h in range(heads) for i in range(blocks)] + [(None, None)] * 2:
        if h is not None:
            scored.append((h, i, scores(h, i)))
        if len(scored) > 1 or (h is None and scored):
            hh, ii, st = scored.pop(0)
            done.append((hh, ii, *attend(hh, ii, st)))
        if len(done) > 1 or (h is None and not scored and done):
            finish(*done.pop(0))
    while done:
        finish(*done.pop(0))


def attend_forward(lengths, q, k, v):
    heads = GROUP
    part = pl.BlockSpec((SEQ, heads * HD), lambda g: (0, g))
    wide = pl.BlockSpec((heads, SEQ, LANES), lambda g: (g, 0, 0))
    return pl.pallas_call(
        functools.partial(forward_kernel, heads),
        grid=(HEADS // heads,),
        in_specs=[pl.BlockSpec(memory_space=pltpu.SMEM), part, part, part],
        out_specs=[part, wide, wide, wide],
        out_shape=[jax.ShapeDtypeStruct((SEQ, D), bf16)]
        + [jax.ShapeDtypeStruct((HEADS, SEQ, LANES), bf16)] * 3,
        compiler_params=pltpu.CompilerParams(vmem_limit_bytes=56 << 20),
        cost_estimate=pl.CostEstimate(
            flops=HEADS * SEQ * SEQ * 1200, bytes_accessed=20 << 20, transcendentals=HEADS * SEQ * SEQ
        ),
        name="attend_forward",
    )(lengths, q, k, v)


def backward_kernel(
    heads, fac_ref, qa_ref, ka_ref, va_ref, o_ref, g_ref, dq_ref, dk_ref, dv_ref, sg_ref, dqs, gs
):
    lane = lax.broadcasted_iota(jnp.int32, (SEQ, LANES), 1)
    causal = lax.broadcasted_iota(jnp.int32, (BLOCK, BLOCK), 0) <= lax.broadcasted_iota(
        jnp.int32, (BLOCK, BLOCK), 1
    )
    fac = fac_ref[0:1, :]
    blocks = SEQ // BLOCK

    @pl.when(pl.program_id(0) == 0)
    def _():
        sg_ref[...] = jnp.zeros_like(sg_ref)

    sums = []

    def prepare(h):
        own = slice(h * HD, (h + 1) * HD)
        g = widen(g_ref[:, own]).astype(f32)
        o = widen(o_ref[:, own]).astype(f32)
        delta = jnp.sum(g * o, axis=1, keepdims=True)
        gs[h] = extra_lanes(lane, g, split3(-delta)).astype(bf16)

    def products(h, j):
        js = slice(j * BLOCK, (j + 1) * BLOCK)
        return nt(ka_ref[h, js, :], qa_ref[h, j * BLOCK :, :]), nt(va_ref[h, js, :], gs[h, j * BLOCK :, :])

    def middle(j, st, dpt):
        p = jnp.exp2(st)
        diagonal = jnp.where(causal, p[:, :BLOCK], 0.0)
        p = jnp.concatenate([diagonal, p[:, BLOCK:]], axis=1) if j < blocks - 1 else diagonal
        return (p * dpt).astype(bf16), p.astype(bf16)

    def finish(h, j, ds, p):
        own = slice(h * HD, (h + 1) * HD)
        js = slice(j * BLOCK, (j + 1) * BLOCK)
        dv_ref[js, own] = nn(p, gs[h, j * BLOCK :, :])[:, :HD].astype(bf16)
        dk_ref[js, own] = (nn(ds, qa_ref[h, j * BLOCK :, :])[:, :HD] * (1.0 / LOG2E)).astype(bf16)
        dqt = tn(ka_ref[h, js, :], ds)
        if j == 0:
            dqs[h % 2] = dqt
        else:
            dqs[h % 2, :, j * BLOCK :] += dqt
        if j == blocks - 1:
            dq = dqs[h % 2].T.astype(bf16).astype(f32)
            sums.append(jnp.sum(dq * qa_ref[h].astype(f32), axis=0, keepdims=True))
            dq_ref[:, own] = (dq * fac)[:, :HD].astype(bf16)

    for h in range(heads):
        prepare(h)
    waiting = []
    for h, j in [(h, j) for h in range(heads) for j in range(blocks)]:
        waiting.append((h, j, *products(h, j)))
        if len(waiting) > 1:
            hh, jj, st, dpt = waiting.pop(0)
            finish(hh, jj, *middle(jj, st, dpt))
    hh, jj, st, dpt = waiting.pop(0)
    finish(hh, jj, *middle(jj, st, dpt))
    sg_ref[0:1, :] += sum(sums)


def attend_backward(fac, qa, ka, va, o, g):
    heads = GROUP
    part = pl.BlockSpec((SEQ, heads * HD), lambda g: (0, g))
    wide = pl.BlockSpec((heads, SEQ, LANES), lambda g: (g, 0, 0))
    full = pl.BlockSpec((8, LANES), lambda g: (0, 0))
    return pl.pallas_call(
        functools.partial(backward_kernel, heads),
        grid=(HEADS // heads,),
        in_specs=[full, wide, wide, wide, part, part],
        out_specs=[part, part, part, full],
        out_shape=[jax.ShapeDtypeStruct((SEQ, D), bf16)] * 3 + [jax.ShapeDtypeStruct((8, LANES), f32)],
        scratch_shapes=[pltpu.VMEM((2, LANES, SEQ), f32), pltpu.VMEM((heads, SEQ, LANES), bf16)],
        compiler_params=pltpu.CompilerParams(vmem_limit_bytes=56 << 20),
        cost_estimate=pl.CostEstimate(
            flops=HEADS * SEQ * SEQ * 2400, bytes_accessed=20 << 20, transcendentals=HEADS * SEQ * SEQ
        ),
        name="attend_backward",
    )(fac, qa, ka, va, o, g)


class Grid:
    def __init__(self, mesh_shape):
        self.copies, self.owners = mesh_shape["replica"], mesh_shape["fsdp"]
        self.planes = self.owners // 2
        self.rows = D // self.owners

    @property
    def pieced(self):
        return self.copies == 4 and self.owners % 2 == 0 and self.rows % 32 == 0 and self.planes <= 4

    def place(self):
        me, copy = lax.axis_index("fsdp"), lax.axis_index("replica")
        return copy // 2, copy % 2, me // 2, me % 2

    def along_z(self, v, step):
        n = self.planes
        pairs = [(i, (i // 2 + step) % n * 2 + i % 2) for i in range(self.owners)]
        return lax.ppermute(v, "fsdp", pairs)

    def other_core(self, v):
        return lax.ppermute(v, "fsdp", [(i, i ^ 1) for i in range(self.owners)])

    def across(self, v, code):
        return lax.ppermute(v, "replica", [(i, i ^ code) for i in range(self.copies)])


def assemble_kernel(count, planes, place_ref, *refs):
    own, other = refs[:5], refs[5:10]
    outs = refs[10 : 10 + count]
    sem = refs[10 + count]
    y, x, z, core = (place_ref[i] for i in range(4))
    rows = D // (2 * planes)
    half = rows // 2
    copies = []
    for source, c in ((own, core), (other, 1 - core)):
        block, along, *crossed = source
        for w in range(count):
            at = pl.multiple_of((2 * z + c) * rows, 16)
            copies.append((block.at[w], outs[w].at[pl.ds(at, rows), :]))
            for d in range(1, planes):
                plane = lax.rem(z - d + planes, planes)
                for code, piece in enumerate((along, *crossed)):
                    py = y if code < 2 else 1 - y
                    px = x if code % 2 == 0 else 1 - x
                    at = pl.multiple_of((2 * plane + c) * rows + py * half, 16)
                    across = pl.multiple_of(px * (D // 2), LANES)
                    copies.append(
                        (piece.at[d - 1, w], outs[w].at[pl.ds(at, half), pl.ds(across, D // 2)])
                    )
    started = []
    for n, (source, target) in enumerate(copies):
        copy = pltpu.make_async_copy(source, target, sem.at[n])
        copy.start()
        started.append(copy)
    for copy in started:
        copy.wait()


def gather_weights(grid, shards, extra=None):
    count = shards.shape[0]
    y, x, z, core = grid.place()
    half = grid.rows // 2
    piece = lax.dynamic_slice(shards, (0, y * half, x * (D // 2)), (count, half, D // 2))
    sent = piece.reshape(count * half, D // 2)
    if extra is not None:
        sent = jnp.concatenate([sent, extra], axis=0)
    arrived = [grid.along_z(sent, d) for d in range(1, grid.planes)]
    along = jnp.stack([a[: count * half] for a in arrived]).reshape(-1, count, half, D // 2)
    crossed = [grid.across(along, code) for code in (1, 2, 3)]
    own = [shards, along, *crossed]
    other = [grid.other_core(v) for v in own]
    place = jnp.stack([y, x, z, core]).astype(jnp.int32)
    total = 2 * count * (1 + 4 * (grid.planes - 1))
    whole = pl.pallas_call(
        functools.partial(assemble_kernel, count, grid.planes),
        in_specs=[pl.BlockSpec(memory_space=pltpu.SMEM)] + [pl.BlockSpec(memory_space=pl.ANY)] * 10,
        out_specs=[pl.BlockSpec(memory_space=pl.ANY)] * count,
        out_shape=[jax.ShapeDtypeStruct((D, D), bf16)] * count,
        scratch_shapes=[pltpu.SemaphoreType.DMA((total,))],
        cost_estimate=pl.CostEstimate(flops=0, bytes_accessed=count * D * D * 4, transcendentals=0),
        name="assemble",
    )(place, *own, *other)
    if extra is None:
        return whole, None
    mine = jnp.stack([extra] + [a[count * half :] for a in arrived])[:, :1]
    theirs = grid.other_core(mine)
    both = jnp.stack([jnp.where(core == 0, mine, theirs), jnp.where(core == 0, theirs, mine)], axis=1)
    planes = jnp.arange(grid.planes)
    ordered = sum(
        jnp.where((planes == (z - d) % grid.planes)[:, None, None, None], both[d][None], 0)
        for d in range(grid.planes)
    )
    return whole, ordered.reshape(grid.owners, D // 2)


def low_sum(*parts):
    total = parts[0].astype(f32)
    for part in parts[1:]:
        total = total + part.astype(f32)
    return total.astype(bf16)


def pick(v, index, axis):
    return lax.dynamic_index_in_dim(v, index, axis, keepdims=False)


def reduce_unit(grid, grads, vectors):
    y, x, z, core = grid.place()
    n, rows, half = grid.planes, grid.rows, grid.rows // 2
    extra = jnp.stack(vectors + [jnp.zeros_like(vectors[0])] * (4 - len(vectors)), axis=1)
    extra = extra.reshape(n, 2, 1, 1, 1, D // 2)
    extra = jnp.broadcast_to(
        jnp.pad(extra, ((0, 0),) * 4 + ((0, 15), (0, 0))), (n, 2, 2, 2, 16, D // 2)
    ).astype(bf16)

    def of_core(c):
        parts = [
            pick(g.reshape(n, 2, 2, half, 2, D // 2), c, 1).transpose(0, 1, 3, 2, 4).astype(bf16)
            for g in grads
        ]
        return jnp.concatenate(parts + [pick(extra, c, 1)], axis=3)

    a = low_sum(of_core(core), grid.other_core(of_core(1 - core)))
    low, high = a[..., :128, :], a[..., 128:, :]
    b1 = low_sum(pick(low, x, 2), grid.across(pick(low, 1 - x, 2), 1))
    b2 = low_sum(pick(high, y, 1), grid.across(pick(high, 1 - y, 1), 2))
    c1 = low_sum(pick(b1, y, 1), grid.across(pick(b1, 1 - y, 1), 2))
    c2 = low_sum(pick(b2, x, 1), grid.across(pick(b2, 1 - x, 1), 1))
    c = jnp.concatenate([c1, c2], axis=1)
    d = low_sum(
        pick(c, z, 0), *[grid.along_z(pick(c, (z + s) % n, 0), s) for s in range(1, n)]
    )
    crossed = [d] + [grid.across(d, code) for code in (1, 2, 3)]

    def at(py, px):
        code = (y != py) * 2 + (x != px)
        out = crossed[0]
        for k in (1, 2, 3):
            out = jnp.where(code == k, crossed[k], out)
        return out

    whole = jnp.concatenate(
        [jnp.concatenate([at(py, 0), at(py, 1)], axis=1)[None] for py in (0, 1)], axis=0
    ).astype(f32)
    out = [whole[:, w * half : (w + 1) * half].reshape(rows, D) for w in range(3)]
    tail = whole[0, 3 * half, : D // 2].reshape(4, rows)
    return out, tail


def shards(
    grid,
    tokens,
    lengths,
    cotangent,
    query_weight,
    key_weight,
    value_weight,
    output_weight,
    up_weight,
    down_weight,
    attn_gain,
    mlp_gain,
    up_bias,
    down_bias,
    query_scale,
):
    vectors = jnp.concatenate([attn_gain, mlp_gain, up_bias, down_bias])
    if grid.pieced:
        extra = jnp.pad(vectors[None], ((0, 15), (0, 0)))
        (wq, wk, wv), vecs = gather_weights(
            grid, jnp.stack([query_weight, key_weight, value_weight]), extra
        )
        (wo, w_up, w_down), _ = gather_weights(grid, jnp.stack([output_weight, up_weight, down_weight]))
        vecs = vecs.reshape(grid.owners, 4, grid.rows)
    else:
        wq, wk, wv, wo, w_up, w_down = (
            lax.all_gather(w, "fsdp", axis=0, tiled=True)
            for w in (query_weight, key_weight, value_weight, output_weight, up_weight, down_weight)
        )
        vecs = lax.all_gather(vectors, "fsdp", axis=0).reshape(grid.owners, 4, grid.rows)
    gain_a, gain_m, bias_up, bias_down = (vecs[:, i].reshape(D).astype(f32) for i in range(4))

    slots = lengths.shape[0]
    xin = tokens.astype(f32)
    normed1, inverse1 = rms_parts(xin)
    attn_in = (normed1 * gain_a).astype(bf16)
    factor = query_scale.astype(f32) * (1.0 / jnp.sqrt(f32(HD)))
    q2 = (nn(attn_in, wq) * jnp.tile(factor * LOG2E, HEADS)).astype(bf16)
    keys = nn(attn_in, wk).astype(bf16)
    values = nn(attn_in, wv).astype(bf16)

    def slot(v, s):
        return v[s * SEQ : (s + 1) * SEQ] if slots > 1 else v

    def joined(parts):
        return jnp.concatenate(parts, axis=0) if slots > 1 else parts[0]

    kept = [
        attend_forward(lengths[s : s + 1], slot(q2, s), slot(keys, s), slot(values, s)) for s in range(slots)
    ]
    attended = joined([k[0] for k in kept])
    hidden1 = xin + nn(attended, wo)
    normed2, inverse2 = rms_parts(hidden1)
    mlp_in = (normed2 * gain_m).astype(bf16)
    pre = nn(mlp_in, w_up) + bias_up
    sigma = jax.nn.sigmoid(pre)
    act = (pre * sigma).astype(bf16)
    out_f = hidden1 + nn(act, w_down) + bias_down

    positions = jnp.arange(SEQ, dtype=jnp.int32)
    valid = (positions[None, :] < lengths[:, None]).reshape(-1, 1).astype(f32)
    grad_out = cotangent.astype(f32) * valid
    grad_out_low = grad_out.astype(bf16)
    down_bias_grad = jnp.sum(grad_out, axis=0)
    grad_pre = (nt(grad_out_low, w_down) * (sigma * (1.0 + pre * (1.0 - sigma)))).astype(bf16)
    up_bias_grad = jnp.sum(grad_pre.astype(f32), axis=0)
    grad_mlp_in = nt(grad_pre, w_up)
    mlp_gain_grad = jnp.sum(grad_mlp_in * normed2, axis=0)
    grad_hidden = grad_out + rms_back(grad_mlp_in * gain_m, normed2, inverse2)
    grad_proj = grad_hidden.astype(bf16)
    grad_att = nt(grad_proj, wo).astype(bf16)

    fac_row = jnp.broadcast_to(jnp.pad(factor, (0, LANES - HD))[None], (8, LANES))
    backs = [
        attend_backward(fac_row, *kept[s][1:], kept[s][0], slot(grad_att, s)) for s in range(slots)
    ]
    grad_query, grad_keys, grad_values = (joined([b[i] for b in backs]) for i in range(3))
    scale_part = sum(b[3][0, :HD] for b in backs) / (query_scale.astype(f32) * LOG2E)
    grad_attn_in = nt(grad_query, wq) + nt(grad_keys, wk) + nt(grad_values, wv)
    attn_gain_grad = jnp.sum(grad_attn_in * normed1, axis=0)
    input_grad = grad_hidden + rms_back(grad_attn_in * gain_a, normed1, inverse1)

    mlp_grads = [tn(attended, grad_proj), tn(mlp_in, grad_pre), tn(act, grad_out_low)]
    attn_grads = [tn(attn_in, g) for g in (grad_query, grad_keys, grad_values)]
    if grid.pieced:
        owned = (grid.owners, grid.rows)
        (g_o, g_up, g_down), tail_m = reduce_unit(
            grid, mlp_grads, [v.reshape(owned) for v in (mlp_gain_grad, up_bias_grad, down_bias_grad)]
        )
        scale_rows = jnp.broadcast_to(jnp.pad(scale_part, (0, grid.rows - HD))[None], owned)
        (g_q, g_k, g_v), tail_a = reduce_unit(grid, attn_grads, [attn_gain_grad.reshape(owned), scale_rows])
        sums = (g_q, g_k, g_v, g_o, g_up, g_down, tail_a[0], tail_m[0], tail_m[1], tail_m[2])
        scale_grad = tail_a[1, :HD]
    else:
        sums = tuple(
            lax.psum(lax.psum_scatter(g, "fsdp", scatter_dimension=0, tiled=True), "replica")
            for g in (*attn_grads, *mlp_grads, attn_gain_grad, mlp_gain_grad, up_bias_grad, down_bias_grad)
        )
        scale_grad = lax.psum(scale_part, ("replica", "fsdp"))
    return (out_f.astype(bf16), input_grad.astype(bf16), *sums, scale_grad)


def solution(mesh):
    split = P(("replica", "fsdp"), None)
    rows = P("fsdp", None)
    part = P("fsdp")
    return jax.shard_map(
        functools.partial(shards, Grid(mesh.shape)),
        mesh=mesh,
        in_specs=(split, P(("replica", "fsdp")), split, *[rows] * 6, *[part] * 4, P()),
        out_specs=(split, split, *[rows] * 6, *[part] * 4, P()),
        check_vma=False,
    )
```

time: 1050 us -> 1200 us (1.14)
  Pallas kernels: 0 us -> 659 us
  waiting for transfers between devices: 426 us -> 161 us
  matrix products: 293 us -> 106 us
  blocking collectives: 110 us -> 0 us
  starting transfers between devices: 0.31 us -> 79.5 us
  other arithmetic: 96 us -> 49.9 us
  local copies, waits for them, and re-layouts: 95.8 us -> 120 us
  between operations: 16.8 us -> 2.73 us
    pallas_call x0 -> x4, Pallas kernels: none -> 659 us  [the longest x2 601 us: gather_weights(): pl.pallas_call(functools.partial(assemble_kernel, count, grid.planes), in...]
    unnamed x9 -> x0, waiting for transfers between devices: 278 us -> none
    dot_general x24 -> x18, matrix products: 293 us -> 106 us  [the longest x6 38.4 us: nt(): lax.dot_general(a, b, (((1,), (1,)), ((), ())), preferred_element_type=f32)]
    ppermute x0 -> x45, waiting for transfers between devices: none -> 161 us  [the longest x20 108 us: across(): lax.ppermute(v, 'replica', [(i, i ^ code) for i in range(self.copies)])]
    psum x1 -> x0, waiting for transfers between devices: 83.1 us -> none  [shards(): lax.psum(owned.astype(jnp.bfloat16), 'replica').astype(jnp.float32)]
    ppermute x0 -> x45, starting transfers between devices: none -> 79.5 us  [the longest x12 50.1 us: along_z(): return lax.ppermute(v, 'fsdp', pairs)]
    all_gather x6 -> x0, waiting for transfers between devices: 65.4 us -> none  [the longest x1 30.4 us: shards(): lax.all_gather(down_weight, 'fsdp', axis=0, tiled=True)]
    unnamed x2 -> x0, blocking collectives: 61.4 us -> none
  transfers between devices with their start and end apart: 8 -> 45, of which waited for: 5 -> 17; matrix products, arithmetic and copies ran while one was open for 18% -> 9% of each run, Pallas kernels for 0% -> 25%
where the time goes in v1:
time: 1200 us; the launch traced here: 1180 us
  Pallas kernels  659 us (55%)
  waiting for transfers between devices  161 us (13%)
  local copies, waits for them, and re-layouts  120 us (10%)
  matrix products  106 us (9%)
  starting transfers between devices  79.5 us (7%)
  other arithmetic  49.9 us (4%)
    pallas_call x2, Pallas kernels, gather_weights(): pl.pallas_call(functools.partial(assemble_kernel, count, grid.planes), in...  601 us
    ppermute x20, waiting for transfers between devices, across(): lax.ppermute(v, 'replica', [(i, i ^ code) for i in range(self.copies)])  108 us
    ppermute x12, waiting for transfers between devices, along_z(): return lax.ppermute(v, 'fsdp', pairs)  53.7 us
    ppermute x12, starting transfers between devices, along_z(): return lax.ppermute(v, 'fsdp', pairs)  50.1 us
    reshape x6, local copies, waits for them, and re-layouts, of_core(): g.reshape(n, 2, 2, half, 2, D // 2)  41.3 us
    dot_general x6, matrix products, nt(): lax.dot_general(a, b, (((1,), (1,)), ((), ())), preferred_element_type=f32)  38.4 us
    pallas_call x1, Pallas kernels, attend_backward(): pl.pallas_call(functools.partial(backward_kernel, heads), grid=(HEADS //...  36.2 us
    dot_general x6, matrix products, nn(): lax.dot_general(a, b, (((1,), (0,)), ((), ())), preferred_element_type=f32)  35.8 us
  transfers between devices with their start and end apart: 45, of which 17 were waited for; matrix products, arithmetic and copies ran while one was open for 9% of the time, Pallas kernels for 25%

profile of v1, /device:TPU:0, one launch (start us, length us, event | category | flops | bytes accessed | tf_op | source)
XLA Modules:
  0.0 1178.5 jit_solution(8649621596309163263)
XLA Ops:
  0.7 2.5 pad_maximum_fusion.3.refs_0_
  4.2 5.1 collective-permute-start.14
  11.4 2.9 collective-permute-start.2
  17.0 12.5 %collective-permute-start = (bf16[256,640]{1,0:T(8,128)(2,1)S(1)}, bf16[256,640]{1,0:T(8,128)(2,1)S(1)}, u32[]{:S(2)}, u32[]{:S(2)}) collective-permute-start(bf16[256,640]{1,0:T(8,128)(2,1)S(1)} %pad_maximum_fusion.6), channel_id=1, source_target_pairs={{0,2},{1,3},{2,4},{3,5},{4,6},{5,7},{6,0},{7,1},{8,10},{9,11},{10,... | collective-permute-start | bytes 983048 | tf_op jit(solution)/shard_map/ppermute | solution.py:245
  29.5 7.9 collective-permute-done.13
  38.1 2.4 collective-permute-start.17
  40.6 23.0 %collective-permute-done.1 = bf16[256,640]{1,0:T(8,128)(2,1)S(1)} collective-permute-done((bf16[256,640]{1,0:T(8,128)(2,1)S(1)}, bf16[256,640]{1,0:T(8,128)(2,1)S(1)}, u32[]{:S(2)}, u32[]{:S(2)}) %collective-permute-start.1) | collective-permute-done | bytes 327712 | tf_op jit(solution)/shard_map/ppermute | solution.py:245
  73.1 13.9 %collective-permute-done.16.refs_3_ = bf16[3,3,80,640]{3,2,1,0:T(8,128)(2,1)} collective-permute-done((bf16[3,3,80,640]{3,2,1,0:T(8,128)(2,1)S(1)}, bf16[3,3,80,640]{3,2,1,0:T(8,128)(2,1)}, u32[]{:S(2)}, u32[]{:S(2)}) %collective-permute-start.16) | collective-permute-done | bytes 921632 | tf_op jit(solution)/shard_map/ppermute | solution.py:251
  89.4 19.6 %collective-permute-done.6.refs_4_ = bf16[3,3,80,640]{3,2,1,0:T(8,128)(2,1)} collective-permute-done((bf16[3,3,80,640]{3,2,1,0:T(8,128)(2,1)}, bf16[3,3,80,640]{3,2,1,0:T(8,128)(2,1)}, u32[]{:S(2)}, u32[]{:S(2)}) %collective-permute-start.6) | collective-permute-done | bytes 921632 | tf_op jit(solution)/shard_map/ppermute | solution.py:251
  111.3 14.8 %collective-permute-done.5.refs_3_ = bf16[3,3,80,640]{3,2,1,0:T(8,128)(2,1)} collective-permute-done((bf16[3,3,80,640]{3,2,1,0:T(8,128)(2,1)}, bf16[3,3,80,640]{3,2,1,0:T(8,128)(2,1)}, u32[]{:S(2)}, u32[]{:S(2)}) %collective-permute-start.5) | collective-permute-done | bytes 921632 | tf_op jit(solution)/shard_map/ppermute | solution.py:251
  156.0 300.3 %assemble.3 = (bf16[1280,1280]{1,0:T(8,128)(2,1)}, bf16[1280,1280]{1,0:T(8,128)(2,1)}, bf16[1280,1280]{1,0:T(8,128)(2,1)}) custom-call(s32[4]{0:T(128)} %pad_add_fusion.place_ref, bf16[3,160,1280]{2,1,0:T(8,128)(2,1)} %pad_maximum_fusion.3.refs_0_, bf16[3,3,80,640]{3,2,1,0:T(8,128)(2,1)} %copy-done.16, ...), custom_call_target="tpu_custom_call" | custom-call | bytes 19660800 | tf_op jit(solution)/shard_map/assemble/pallas_call | solution.py:301
  457.2 300.3 %assemble.2 = (bf16[1280,1280]{1,0:T(8,128)(2,1)}, bf16[1280,1280]{1,0:T(8,128)(2,1)}, bf16[1280,1280]{1,0:T(8,128)(2,1)}) custom-call(s32[4]{0:T(128)} %pad_add_fusion.place_ref, bf16[3,160,1280]{2,1,0:T(8,128)(2,1)} %copy-done.14, bf16[3,3,80,640]{3,2,1,0:T(8,128)(2,1)} %pad_maximum_fusion.4.refs_1_, ...), custom_call_target="tpu_custom_call" | custom-call | bytes 19660800 | tf_op jit(solution)/shard_map/assemble/pallas_call | solution.py:301
  757.5 7.1 convolution_convert_fusion.2.k_ref
  764.7 5.0 convolution_convert_fusion.1.v_ref
  769.7 5.0 multiply_convert_fusion.3.q_ref
  774.8 22.3 %attend_forward.1 = (bf16[1024,1280]{1,0:T(8,128)(2,1)}, bf16[16,1024,128]{2,1,0:T(8,128)(2,1)}, bf16[16,1024,128]{2,1,0:T(8,128)(2,1)}, bf16[16,1024,128]{2,1,0:T(8,128)(2,1)}) custom-call(s32[1]{0:T(128)} %copy.180.len_ref, bf16[1024,1280]{1,0:T(8,128)(2,1)} %multiply_convert_fusion.3.q_ref, bf16[1024,1280]{1,0:T(8,128)(2,1)} %convolution_convert_fusion.2.k_ref, ...), custom_call_target="tpu_custom_call" | custom-call | flops 20132659200 | bytes 20971520 | tf_op jit(solution)/shard_map/attend_forward/pallas_call | solution.py:132
  797.1 5.6 multiply_reduce_fusion.2
  802.7 3.7 fusion.71
  806.4 5.6 fusion.37
  812.1 8.3 fusion.85
  820.3 5.9 multiply_reduce_fusion
  826.2 5.3 fusion.70
  831.6 2.1 fusion.12
  833.7 4.9 convolution_convert_fusion.g_ref
  838.7 5.1 fusion.34
  844.4 36.2 %attend_backward.1 = (bf16[1024,1280]{1,0:T(8,128)(2,1)}, bf16[1024,1280]{1,0:T(8,128)(2,1)}, bf16[1024,1280]{1,0:T(8,128)(2,1)}, f32[8,128]{1,0:T(8,128)}) custom-call(f32[8,128]{1,0:T(8,128)} %broadcast_in_dim.171.fac_ref, bf16[16,1024,128]{2,1,0:T(8,128)(2,1)} %get-tuple-element.34.qa_ref, bf16[16,1024,128]{2,1,0:T(8,128)(2,1)} %get-tuple-element.35.ka_ref, ...), custom_call_target="tpu_custom_call" | custom-call | flops 40265318400 | bytes 20971520 | tf_op jit(solution)/shard_map/attend_backward/pallas_call | solution.py:213
  880.6 7.8 fusion.86
  888.4 5.2 fusion.76
  893.7 5.3 fusion.87
  899.0 5.2 fusion.74
  904.3 6.2 reshape.277
  911.1 7.2 reshape.268
  918.4 5.5 constant_dynamic-slice_fusion.11
  926.2 5.5 fusion.72
  931.8 6.2 fusion.10
  938.5 7.2 reshape.270
  945.7 5.9 constant_dynamic-slice_fusion.9
  951.6 7.2 reshape.269
  958.9 5.3 constant_dynamic-slice_fusion.10
  966.1 6.0 pad_maximum_fusion
  972.4 4.0 constant_dynamic-slice_fusion.3
  976.5 2.8 copy.171
  979.4 6.2 reshape.276
  986.7 7.2 reshape.275
  993.9 5.3 constant_dynamic-slice_fusion.5
  999.4 3.4 constant_dynamic-slice_fusion.4
  1004.3 5.9 pad_maximum_fusion.1
  1015.0 6.5 add_convert_fusion.1
  1025.8 6.8 add_convert_fusion
  1034.9 9.3 add_convert_fusion.2
  1044.2 9.9 collective-permute-done.24
  1058.1 24.1 %collective-permute-done.35 = bf16[4,2,128,640]{3,2,0,1:T(8,128)(2,1)S(1)} collective-permute-done((bf16[4,2,128,640]{3,2,0,1:T(8,128)(2,1)S(1)}, bf16[4,2,128,640]{3,2,0,1:T(8,128)(2,1)S(1)}, u32[]{:S(2)}, u32[]{:S(2)}) %collective-permute-start.35) | collective-permute-done | bytes 1310752 | tf_op jit(solution)/shard_map/ppermute | solution.py:251
  1086.3 11.7 collective-permute-done.25
  1098.5 12.6 %collective-permute-start.28 = (bf16[256,640]{1,0:T(8,128)(2,1)S(1)}, bf16[256,640]{1,0:T(8,128)(2,1)S(1)}, u32[]{:S(2)}, u32[]{:S(2)}) collective-permute-start(bf16[256,640]{1,0:T(8,128)(2,1)S(1)} %get-tuple-element.88), channel_id=1, source_target_pairs={{0,2},{1,3},{2,4},{3,5},{4,6},{5,7},{6,0},{7,1},{8,10},{9,11},{10,... | collective-permute-start | bytes 983048 | tf_op jit(solution)/shard_map/ppermute | solution.py:245
  1111.1 2.4 collective-permute-start.30
  1114.0 10.0 collective-permute-start.39
  1123.9 2.4 collective-permute-start.41
  1126.4 10.5 collective-permute-done.29
  1141.9 2.7 fusion.9
  1144.6 9.5 collective-permute-done.40
  1158.9 6.0 collective-permute-done.44
  1164.9 5.3 collective-permute-done.43
  1170.2 1.6 collective-permute-done.42
  1172.8 1.7 maximum_convert_fusion.1
  (333 shorter events, 94.4 us)
Async XLA Ops:
  0.6 10.5 copy-start.21
  0.7 10.5 copy-start.22
  0.7 10.5 copy-start.23
  4.2 12.8 %collective-permute-start.14 = (bf16[240,640]{1,0:T(8,128)(2,1)S(1)}, bf16[240,640]{1,0:T(8,128)(2,1)S(1)}, u32[]{:S(2)}, u32[]{:S(2)}) collective-permute-start(bf16[240,640]{1,0:T(8,128)(2,1)S(1)} %bitcast.264), channel_id=1, source_target_pairs={{0,6},{1,7},{2,0},{3,1},{4,2},{5,3},{6,4},{7,5},{8,14},{9,15},{10,... | collective-permute-start | bytes 921608 | tf_op jit(solution)/shard_map/ppermute | solution.py:245
  9.3 28.1 %collective-permute-start.13 = (bf16[240,640]{1,0:T(8,128)(2,1)S(1)}, bf16[240,640]{1,0:T(8,128)(2,1)S(1)}, u32[]{:S(2)}, u32[]{:S(2)}) collective-permute-start(bf16[240,640]{1,0:T(8,128)(2,1)S(1)} %bitcast.265), channel_id=1, source_target_pairs={{0,4},{1,5},{2,6},{3,7},{4,0},{5,1},{6,2},{7,3},{8,12},{9,13},{10,... | collective-permute-start | bytes 921608 | tf_op jit(solution)/shard_map/ppermute | solution.py:245
  9.3 28.1 %collective-permute-start.12 = (bf16[240,640]{1,0:T(8,128)(2,1)S(1)}, bf16[240,640]{1,0:T(8,128)(2,1)S(1)}, u32[]{:S(2)}, u32[]{:S(2)}) collective-permute-start(bf16[240,640]{1,0:T(8,128)(2,1)S(1)} %bitcast.266), channel_id=1, source_target_pairs={{0,2},{1,3},{2,4},{3,5},{4,6},{5,7},{6,0},{7,1},{8,10},{9,11},{10,... | collective-permute-start | bytes 921608 | tf_op jit(solution)/shard_map/ppermute | solution.py:245
  11.3 56.7 %copy-start.14 = (bf16[3,160,1280]{2,1,0:T(8,128)(2,1)}, bf16[3,160,1280]{2,1,0:T(8,128)(2,1)S(1)}, u32[]{:S(2)}) copy-start(bf16[3,160,1280]{2,1,0:T(8,128)(2,1)S(1)} %pad_maximum_fusion.2.refs_0_) | copy-start | bytes 3686404
  11.4 98.7 %copy-start.1 = (bf16[1024,1280]{1,0:T(8,128)(2,1)S(1)}, bf16[1024,1280]{1,0:T(8,128)(2,1)}, u32[]{:S(2)}) copy-start(bf16[1024,1280]{1,0:T(8,128)(2,1)} %param.14) | copy-start | bytes 7864324
  11.4 26.7 %collective-permute-start.2 = (bf16[256,640]{1,0:T(8,128)(2,1)S(1)}, bf16[256,640]{1,0:T(8,128)(2,1)S(1)}, u32[]{:S(2)}, u32[]{:S(2)}) collective-permute-start(bf16[256,640]{1,0:T(8,128)(2,1)S(1)} %pad_maximum_fusion.6), channel_id=1, source_target_pairs={{0,6},{1,7},{2,0},{3,1},{4,2},{5,3},{6,4},{7,5},{8,14},{9,15},{10,... | collective-permute-start | bytes 983048 | tf_op jit(solution)/shard_map/ppermute | solution.py:245
  14.3 49.3 %collective-permute-start.1 = (bf16[256,640]{1,0:T(8,128)(2,1)S(1)}, bf16[256,640]{1,0:T(8,128)(2,1)S(1)}, u32[]{:S(2)}, u32[]{:S(2)}) collective-permute-start(bf16[256,640]{1,0:T(8,128)(2,1)S(1)} %pad_maximum_fusion.6), channel_id=1, source_target_pairs={{0,4},{1,5},{2,6},{3,7},{4,0},{5,1},{6,2},{7,3},{8,12},{9,13},{10,... | collective-permute-start | bytes 983048 | tf_op jit(solution)/shard_map/ppermute | solution.py:245
  17.0 46.5 %collective-permute-start = (bf16[256,640]{1,0:T(8,128)(2,1)S(1)}, bf16[256,640]{1,0:T(8,128)(2,1)S(1)}, u32[]{:S(2)}, u32[]{:S(2)}) collective-permute-start(bf16[256,640]{1,0:T(8,128)(2,1)S(1)} %pad_maximum_fusion.6), channel_id=1, source_target_pairs={{0,2},{1,3},{2,4},{3,5},{4,6},{5,7},{6,0},{7,1},{8,10},{9,11},{10,... | collective-permute-start | bytes 983048 | tf_op jit(solution)/shard_map/ppermute | solution.py:245
  37.4 51.4 %collective-permute-start.18 = (bf16[3,160,1280]{2,1,0:T(8,128)(2,1)}, bf16[3,160,1280]{2,1,0:T(8,128)(2,1)}, u32[]{:S(2)}, u32[]{:S(2)}) collective-permute-start(bf16[3,160,1280]{2,1,0:T(8,128)(2,1)} %pad_maximum_fusion.3.refs_0_), channel_id=1, source_target_pairs={{0,1},{1,0},{2,3},{3,2},{4,5},{5,4},{6,7},{7,6},{8,9},{9,8},{10,11... | collective-permute-start | bytes 3686408 | tf_op jit(solution)/shard_map/ppermute | solution.py:248
  37.6 73.1 %copy-start.16 = (bf16[3,3,80,640]{3,2,1,0:T(8,128)(2,1)}, bf16[3,3,80,640]{3,2,1,0:T(8,128)(2,1)S(1)}, u32[]{:S(2)}) copy-start(bf16[3,3,80,640]{3,2,1,0:T(8,128)(2,1)S(1)} %pad_maximum_fusion.5.refs_1_) | copy-start | bytes 2764804
  37.6 30.4 %collective-permute-start.19 = (bf16[3,3,80,640]{3,2,1,0:T(8,128)(2,1)S(1)}, bf16[3,3,80,640]{3,2,1,0:T(8,128)(2,1)S(1)}, u32[]{:S(2)}, u32[]{:S(2)}) collective-permute-start(bf16[3,3,80,640]{3,2,1,0:T(8,128)(2,1)S(1)} %pad_maximum_fusion.5.refs_1_), channel_id=1, source_target_pairs={{0,1},{1,0},{2,3},{3,2},{4,5},{5,4},{6,7},{7,6},{8,9},{9,8},{10,11... | collective-permute-start | bytes 2764808 | tf_op jit(solution)/shard_map/ppermute | solution.py:248
  38.1 32.8 %collective-permute-start.17 = (bf16[3,3,80,640]{3,2,1,0:T(8,128)(2,1)S(1)}, bf16[3,3,80,640]{3,2,1,0:T(8,128)(2,1)}, u32[]{:S(2)}, u32[]{:S(2)}) collective-permute-start(bf16[3,3,80,640]{3,2,1,0:T(8,128)(2,1)S(1)} %pad_maximum_fusion.5.refs_1_), channel_id=1, source_target_pairs={{0,24},{8,16},{16,8},{24,0},{1,25},{9,17},{17,9},{25,1},{2,26},{10... | collective-permute-start | bytes 2764808 | tf_op jit(solution)/shard_map/ppermute | solution.py:251
  63.6 1.8 collective-permute-start.3
  63.7 23.4 %collective-permute-start.16 = (bf16[3,3,80,640]{3,2,1,0:T(8,128)(2,1)S(1)}, bf16[3,3,80,640]{3,2,1,0:T(8,128)(2,1)}, u32[]{:S(2)}, u32[]{:S(2)}) collective-permute-start(bf16[3,3,80,640]{3,2,1,0:T(8,128)(2,1)S(1)} %pad_maximum_fusion.5.refs_1_), channel_id=1, source_target_pairs={{0,16},{8,24},{16,0},{24,8},{1,17},{9,25},{17,1},{25,9},{2,18},{10... | collective-permute-start | bytes 2764808 | tf_op jit(solution)/shard_map/ppermute | solution.py:251
  65.4 23.5 %collective-permute-start.15 = (bf16[3,3,80,640]{3,2,1,0:T(8,128)(2,1)S(1)}, bf16[3,3,80,640]{3,2,1,0:T(8,128)(2,1)}, u32[]{:S(2)}, u32[]{:S(2)}) collective-permute-start(bf16[3,3,80,640]{3,2,1,0:T(8,128)(2,1)S(1)} %pad_maximum_fusion.5.refs_1_), channel_id=1, source_target_pairs={{0,8},{8,0},{16,24},{24,16},{1,9},{9,1},{17,25},{25,17},{2,10},{10... | collective-permute-start | bytes 2764808 | tf_op jit(solution)/shard_map/ppermute | solution.py:251
  68.9 40.1 %collective-permute-start.6 = (bf16[3,3,80,640]{3,2,1,0:T(8,128)(2,1)}, bf16[3,3,80,640]{3,2,1,0:T(8,128)(2,1)}, u32[]{:S(2)}, u32[]{:S(2)}) collective-permute-start(bf16[3,3,80,640]{3,2,1,0:T(8,128)(2,1)} %pad_maximum_fusion.4.refs_1_), channel_id=1, source_target_pairs={{0,24},{8,16},{16,8},{24,0},{1,25},{9,17},{17,9},{25,1},{2,26},{10... | collective-permute-start | bytes 2764808 | tf_op jit(solution)/shard_map/ppermute | solution.py:251
  71.0 55.2 %collective-permute-start.5 = (bf16[3,3,80,640]{3,2,1,0:T(8,128)(2,1)}, bf16[3,3,80,640]{3,2,1,0:T(8,128)(2,1)}, u32[]{:S(2)}, u32[]{:S(2)}) collective-permute-start(bf16[3,3,80,640]{3,2,1,0:T(8,128)(2,1)} %pad_maximum_fusion.4.refs_1_), channel_id=1, source_target_pairs={{0,16},{8,24},{16,0},{24,8},{1,17},{9,25},{17,1},{25,9},{2,18},{10... | collective-permute-start | bytes 2764808 | tf_op jit(solution)/shard_map/ppermute | solution.py:251
  87.1 40.5 %collective-permute-start.4 = (bf16[3,3,80,640]{3,2,1,0:T(8,128)(2,1)}, bf16[3,3,80,640]{3,2,1,0:T(8,128)(2,1)}, u32[]{:S(2)}, u32[]{:S(2)}) collective-permute-start(bf16[3,3,80,640]{3,2,1,0:T(8,128)(2,1)} %pad_maximum_fusion.4.refs_1_), channel_id=1, source_target_pairs={{0,8},{8,0},{16,24},{24,16},{1,9},{9,1},{17,25},{25,17},{2,10},{10... | collective-permute-start | bytes 2764808 | tf_op jit(solution)/shard_map/ppermute | solution.py:251
  88.8 39.0 %collective-permute-start.22 = (bf16[3,3,80,640]{3,2,1,0:T(8,128)(2,1)}, bf16[3,3,80,640]{3,2,1,0:T(8,128)(2,1)}, u32[]{:S(2)}, u32[]{:S(2)}) collective-permute-start(bf16[3,3,80,640]{3,2,1,0:T(8,128)(2,1)} %collective-permute-done.17.refs_4_), channel_id=1, source_target_pairs={{0,1},{1,0},{2,3},{3,2},{4,5},{5,4},{6,7},{7,6},{8,9},{9,8},{10,11... | collective-permute-start | bytes 2764808 | tf_op jit(solution)/shard_map/ppermute | solution.py:248
  88.9 39.3 %collective-permute-start.21 = (bf16[3,3,80,640]{3,2,1,0:T(8,128)(2,1)}, bf16[3,3,80,640]{3,2,1,0:T(8,128)(2,1)}, u32[]{:S(2)}, u32[]{:S(2)}) collective-permute-start(bf16[3,3,80,640]{3,2,1,0:T(8,128)(2,1)} %collective-permute-done.16.refs_3_), channel_id=1, source_target_pairs={{0,1},{1,0},{2,3},{3,2},{4,5},{5,4},{6,7},{7,6},{8,9},{9,8},{10,11... | collective-permute-start | bytes 2764808 | tf_op jit(solution)/shard_map/ppermute | solution.py:248
  109.0 19.4 %collective-permute-start.20 = (bf16[3,3,80,640]{3,2,1,0:T(8,128)(2,1)}, bf16[3,3,80,640]{3,2,1,0:T(8,128)(2,1)}, u32[]{:S(2)}, u32[]{:S(2)}) collective-permute-start(bf16[3,3,80,640]{3,2,1,0:T(8,128)(2,1)} %collective-permute-done.15.refs_2_), channel_id=1, source_target_pairs={{0,1},{1,0},{2,3},{3,2},{4,5},{5,4},{6,7},{7,6},{8,9},{9,8},{10,11... | collective-permute-start | bytes 2764808 | tf_op jit(solution)/shard_map/ppermute | solution.py:248
  126.1 330.1 %collective-permute-start.7 = (bf16[3,160,1280]{2,1,0:T(8,128)(2,1)}, bf16[3,160,1280]{2,1,0:T(8,128)(2,1)}, u32[]{:S(2)}, u32[]{:S(2)}) collective-permute-start(bf16[3,160,1280]{2,1,0:T(8,128)(2,1)} %copy-done.14), channel_id=1, source_target_pairs={{0,1},{1,0},{2,3},{3,2},{4,5},{5,4},{6,7},{7,6},{8,9},{9,8},{10,11... | collective-permute-start | bytes 3686408 | tf_op jit(solution)/shard_map/ppermute | solution.py:248
  127.6 328.6 %collective-permute-start.8 = (bf16[3,3,80,640]{3,2,1,0:T(8,128)(2,1)}, bf16[3,3,80,640]{3,2,1,0:T(8,128)(2,1)S(1)}, u32[]{:S(2)}, u32[]{:S(2)}) collective-permute-start(bf16[3,3,80,640]{3,2,1,0:T(8,128)(2,1)} %pad_maximum_fusion.4.refs_1_), channel_id=1, source_target_pairs={{0,1},{1,0},{2,3},{3,2},{4,5},{5,4},{6,7},{7,6},{8,9},{9,8},{10,11... | collective-permute-start | bytes 2764808 | tf_op jit(solution)/shard_map/ppermute | solution.py:248
  127.8 328.5 %collective-permute-start.11 = (bf16[3,3,80,640]{3,2,1,0:T(8,128)(2,1)}, bf16[3,3,80,640]{3,2,1,0:T(8,128)(2,1)}, u32[]{:S(2)}, u32[]{:S(2)}) collective-permute-start(bf16[3,3,80,640]{3,2,1,0:T(8,128)(2,1)} %collective-permute-done.6.refs_4_), channel_id=1, source_target_pairs={{0,1},{1,0},{2,3},{3,2},{4,5},{5,4},{6,7},{7,6},{8,9},{9,8},{10,11... | collective-permute-start | bytes 2764808 | tf_op jit(solution)/shard_map/ppermute | solution.py:248
  128.1 328.2 %collective-permute-start.10 = (bf16[3,3,80,640]{3,2,1,0:T(8,128)(2,1)}, bf16[3,3,80,640]{3,2,1,0:T(8,128)(2,1)}, u32[]{:S(2)}, u32[]{:S(2)}) collective-permute-start(bf16[3,3,80,640]{3,2,1,0:T(8,128)(2,1)} %collective-permute-done.5.refs_3_), channel_id=1, source_target_pairs={{0,1},{1,0},{2,3},{3,2},{4,5},{5,4},{6,7},{7,6},{8,9},{9,8},{10,11... | collective-permute-start | bytes 2764808 | tf_op jit(solution)/shard_map/ppermute | solution.py:248
  128.4 328.0 %collective-permute-start.9 = (bf16[3,3,80,640]{3,2,1,0:T(8,128)(2,1)}, bf16[3,3,80,640]{3,2,1,0:T(8,128)(2,1)}, u32[]{:S(2)}, u32[]{:S(2)}) collective-permute-start(bf16[3,3,80,640]{3,2,1,0:T(8,128)(2,1)} %collective-permute-done.4.refs_2_), channel_id=1, source_target_pairs={{0,1},{1,0},{2,3},{3,2},{4,5},{5,4},{6,7},{7,6},{8,9},{9,8},{10,11... | collective-permute-start | bytes 2764808 | tf_op jit(solution)/shard_map/ppermute | solution.py:248
  456.2 301.2 %copy-start.27 = (f32[1024]{0:T(1024)S(1)}, f32[1024]{0:T(1024)}, u32[]{:S(2)}) copy-start(f32[1024]{0:T(1024)} %add_rsqrt_fusion.1) | copy-start | bytes 12292
  774.8 22.3 %copy-start.41 = (bf16[1280,1280]{1,0:T(8,128)(2,1)S(1)}, bf16[1280,1280]{1,0:T(8,128)(2,1)}, u32[]{:S(2)}) copy-start(bf16[1280,1280]{1,0:T(8,128)(2,1)} %get-tuple-element.31) | copy-start | bytes 9830404
  802.7 28.9 %copy-start.15 = (f32[1024,1280]{1,0:T(8,128)}, f32[1024,1280]{1,0:T(8,128)S(1)}, u32[]{:S(2)}) copy-start(f32[1024,1280]{1,0:T(8,128)S(1)} %get-tuple-element.106) | copy-start | bytes 15728644
  844.4 36.2 %copy-start.44 = (bf16[1280,1280]{1,0:T(8,128)(2,1)S(1)}, bf16[1280,1280]{1,0:T(8,128)(2,1)}, u32[]{:S(2)}) copy-start(bf16[1280,1280]{1,0:T(8,128)(2,1)} %get-tuple-element.27) | copy-start | bytes 9830404
  880.6 7.8 copy-start.25
  923.9 7.8 slice-start.6
  923.9 7.8 slice-start.8
  972.2 42.8 %collective-permute-start.23 = (bf16[4,2,2,256,640]{4,3,0,1,2:T(8,128)(2,1)}, bf16[4,2,2,256,640]{4,3,0,1,2:T(8,128)(2,1)}, u32[]{:S(2)}, u32[]{:S(2)}) collective-permute-start(bf16[4,2,2,256,640]{4,3,0,1,2:T(8,128)(2,1)} %pad_maximum_fusion), channel_id=1, source_target_pairs={{0,1},{1,0},{2,3},{3,2},{4,5},{5,4},{6,7},{7,6},{8,9},{9,8},{10,11... | collective-permute-start | bytes 15728648 | tf_op jit(solution)/shard_map/ppermute | solution.py:248
  1010.2 15.5 %collective-permute-start.34 = (bf16[4,2,2,256,640]{4,3,0,2,1:T(8,128)(2,1)}, bf16[4,2,2,256,640]{4,3,0,2,1:T(8,128)(2,1)}, u32[]{:S(2)}, u32[]{:S(2)}) collective-permute-start(bf16[4,2,2,256,640]{4,3,0,2,1:T(8,128)(2,1)} %pad_maximum_fusion.1), channel_id=1, source_target_pairs={{0,1},{1,0},{2,3},{3,2},{4,5},{5,4},{6,7},{7,6},{8,9},{9,8},{10,11... | collective-permute-start | bytes 15728648 | tf_op jit(solution)/shard_map/ppermute | solution.py:248
  1022.5 31.7 %collective-permute-start.24 = (bf16[4,2,128,640]{3,2,0,1:T(8,128)(2,1)S(1)}, bf16[4,2,128,640]{3,2,0,1:T(8,128)(2,1)S(1)}, u32[]{:S(2)}, u32[]{:S(2)}) collective-permute-start(bf16[4,2,128,640]{3,2,0,1:T(8,128)(2,1)S(1)} %dynamic-slice_bitcast_fusion.3), channel_id=1, source_target_pairs={{0,8},{8,0},{16,24},{24,16},{1,9},{9,1},{17,25},{25,17},{2,10},{10... | collective-permute-start | bytes 3932168 | tf_op jit(solution)/shard_map/ppermute | solution.py:251
  1024.1 32.0 %collective-permute-start.26 = (bf16[4,2,128,640]{3,2,0,1:T(8,128)(2,1)S(1)}, bf16[4,2,128,640]{3,2,0,1:T(8,128)(2,1)S(1)}, u32[]{:S(2)}, u32[]{:S(2)}) collective-permute-start(bf16[4,2,128,640]{3,2,0,1:T(8,128)(2,1)S(1)} %dynamic-slice_bitcast_fusion.2), channel_id=1, source_target_pairs={{0,16},{8,24},{16,0},{24,8},{1,17},{9,25},{17,1},{25,9},{2,18},{10... | collective-permute-start | bytes 3932168 | tf_op jit(solution)/shard_map/ppermute | solution.py:251
  1025.8 9.1 slice-start.2
  1033.7 48.5 %collective-permute-start.35 = (bf16[4,2,128,640]{3,2,0,1:T(8,128)(2,1)S(1)}, bf16[4,2,128,640]{3,2,0,1:T(8,128)(2,1)S(1)}, u32[]{:S(2)}, u32[]{:S(2)}) collective-permute-start(bf16[4,2,128,640]{3,2,0,1:T(8,128)(2,1)S(1)} %dynamic-slice_bitcast_fusion.1), channel_id=1, source_target_pairs={{0,8},{8,0},{16,24},{24,16},{1,9},{9,1},{17,25},{25,17},{2,10},{10... | collective-permute-start | bytes 3932168 | tf_op jit(solution)/shard_map/ppermute | solution.py:251
  1034.3 49.9 %collective-permute-start.37 = (bf16[4,2,128,640]{3,2,0,1:T(8,128)(2,1)S(1)}, bf16[4,2,128,640]{3,2,0,1:T(8,128)(2,1)S(1)}, u32[]{:S(2)}, u32[]{:S(2)}) collective-permute-start(bf16[4,2,128,640]{3,2,0,1:T(8,128)(2,1)S(1)} %dynamic-slice_bitcast_fusion), channel_id=1, source_target_pairs={{0,16},{8,24},{16,0},{24,8},{1,17},{9,25},{17,1},{25,9},{2,18},{10... | collective-permute-start | bytes 3932168 | tf_op jit(solution)/shard_map/ppermute | solution.py:251
  1054.6 43.4 %collective-permute-start.25 = (bf16[4,128,640]{2,1,0:T(8,128)(2,1)S(1)}, bf16[4,128,640]{2,1,0:T(8,128)(2,1)S(1)}, u32[]{:S(2)}, u32[]{:S(2)}) collective-permute-start(bf16[4,128,640]{2,1,0:T(8,128)(2,1)S(1)} %dynamic-slice_bitcast_fusion.7), channel_id=1, source_target_pairs={{0,16},{8,24},{16,0},{24,8},{1,17},{9,25},{17,1},{25,9},{2,18},{10... | collective-permute-start | bytes 1966088 | tf_op jit(solution)/shard_map/ppermute | solution.py:251
  1056.2 85.7 %slice-start.4 = ((s8[5242880]{0:T(1024)(128)(4,1)}), s8[1048576]{0:T(1024)(128)(4,1)S(1)}, s32[]{:S(2)}) async-start(s8[5242880]{0:T(1024)(128)(4,1)} %bitcast.239), calls=%async_computation.4 | async-start | bytes 2097152
  1056.6 41.6 %collective-permute-start.27 = (bf16[4,128,640]{2,1,0:T(8,128)(2,1)S(1)}, bf16[4,128,640]{2,1,0:T(8,128)(2,1)S(1)}, u32[]{:S(2)}, u32[]{:S(2)}) collective-permute-start(bf16[4,128,640]{2,1,0:T(8,128)(2,1)S(1)} %dynamic-slice_bitcast_fusion.6), channel_id=1, source_target_pairs={{0,8},{8,0},{16,24},{24,16},{1,9},{9,1},{17,25},{25,17},{2,10},{10... | collective-permute-start | bytes 1966088 | tf_op jit(solution)/shard_map/ppermute | solution.py:251
  1082.7 30.8 %collective-permute-start.36 = (bf16[4,128,640]{2,1,0:T(8,128)(2,1)S(1)}, bf16[4,128,640]{2,1,0:T(8,128)(2,1)S(1)}, u32[]{:S(2)}, u32[]{:S(2)}) collective-permute-start(bf16[4,128,640]{2,1,0:T(8,128)(2,1)S(1)} %dynamic-slice_bitcast_fusion.5), channel_id=1, source_target_pairs={{0,16},{8,24},{16,0},{24,8},{1,17},{9,25},{17,1},{25,9},{2,18},{10... | collective-permute-start | bytes 1966088 | tf_op jit(solution)/shard_map/ppermute | solution.py:251
  1084.6 57.2 %slice-start.5 = ((s8[5242880]{0:T(1024)(128)(4,1)}), s8[4194304]{0:T(1024)(128)(4,1)S(1)}, s32[]{:S(2)}) async-start(s8[5242880]{0:T(1024)(128)(4,1)} %bitcast.239), calls=%async_computation.5 | async-start | bytes 8388608
  1084.7 29.0 %collective-permute-start.38 = (bf16[4,128,640]{2,1,0:T(8,128)(2,1)S(1)}, bf16[4,128,640]{2,1,0:T(8,128)(2,1)S(1)}, u32[]{:S(2)}, u32[]{:S(2)}) collective-permute-start(bf16[4,128,640]{2,1,0:T(8,128)(2,1)S(1)} %dynamic-slice_bitcast_fusion.4), channel_id=1, source_target_pairs={{0,8},{8,0},{16,24},{24,16},{1,9},{9,1},{17,25},{25,17},{2,10},{10... | collective-permute-start | bytes 1966088 | tf_op jit(solution)/shard_map/ppermute | solution.py:251
  1098.0 43.9 %slice-start = ((s8[5242880]{0:T(1024)(128)(4,1)}), s8[4194304]{0:T(1024)(128)(4,1)S(1)}, s32[]{:S(2)}) async-start(s8[5242880]{0:T(1024)(128)(4,1)} %bitcast.223), calls=%async_computation | async-start | bytes 8388608
  1098.5 25.5 %collective-permute-start.28 = (bf16[256,640]{1,0:T(8,128)(2,1)S(1)}, bf16[256,640]{1,0:T(8,128)(2,1)S(1)}, u32[]{:S(2)}, u32[]{:S(2)}) collective-permute-start(bf16[256,640]{1,0:T(8,128)(2,1)S(1)} %get-tuple-element.88), channel_id=1, source_target_pairs={{0,2},{1,3},{2,4},{3,5},{4,6},{5,7},{6,0},{7,1},{8,10},{9,11},{10,... | collective-permute-start | bytes 983048 | tf_op jit(solution)/shard_map/ppermute | solution.py:245
  1111.1 25.8 %collective-permute-start.29 = (bf16[256,640]{1,0:T(8,128)(2,1)S(1)}, bf16[256,640]{1,0:T(8,128)(2,1)S(1)}, u32[]{:S(2)}, u32[]{:S(2)}) collective-permute-start(bf16[256,640]{1,0:T(8,128)(2,1)S(1)} %get-tuple-element.89), channel_id=1, source_target_pairs={{0,4},{1,5},{2,6},{3,7},{4,0},{5,1},{6,2},{7,3},{8,12},{9,13},{10,... | collective-permute-start | bytes 983048 | tf_op jit(solution)/shard_map/ppermute | solution.py:245
  1111.1 30.8 %slice-start.1 = ((s8[5242880]{0:T(1024)(128)(4,1)}), s8[1048576]{0:T(1024)(128)(4,1)S(1)}, s32[]{:S(2)}) async-start(s8[5242880]{0:T(1024)(128)(4,1)} %bitcast.223), calls=%async_computation.1 | async-start | bytes 2097152
  1111.1 25.8 %collective-permute-start.30 = (bf16[256,640]{1,0:T(8,128)(2,1)S(1)}, bf16[256,640]{1,0:T(8,128)(2,1)S(1)}, u32[]{:S(2)}, u32[]{:S(2)}) collective-permute-start(bf16[256,640]{1,0:T(8,128)(2,1)S(1)} %get-tuple-element.90), channel_id=1, source_target_pairs={{0,6},{1,7},{2,0},{3,1},{4,2},{5,3},{6,4},{7,5},{8,14},{9,15},{10,... | collective-permute-start | bytes 983048 | tf_op jit(solution)/shard_map/ppermute | solution.py:245
  1113.7 28.2 %copy-start.3 = (bf16[1024,1280]{1,0:T(8,128)(2,1)S(1)}, bf16[1024,1280]{1,0:T(8,128)(2,1)}, u32[]{:S(2)}) copy-start(bf16[1024,1280]{1,0:T(8,128)(2,1)} %param.14) | copy-start | bytes 7864324
  1114.0 26.4 %collective-permute-start.39 = (bf16[256,640]{1,0:T(8,128)(2,1)S(1)}, bf16[256,640]{1,0:T(8,128)(2,1)S(1)}, u32[]{:S(2)}, u32[]{:S(2)}) collective-permute-start(bf16[256,640]{1,0:T(8,128)(2,1)S(1)} %get-tuple-element.81), channel_id=1, source_target_pairs={{0,2},{1,3},{2,4},{3,5},{4,6},{5,7},{6,0},{7,1},{8,10},{9,11},{10,... | collective-permute-start | bytes 983048 | tf_op jit(solution)/shard_map/ppermute | solution.py:245
  1123.9 30.1 %collective-permute-start.40 = (bf16[256,640]{1,0:T(8,128)(2,1)S(1)}, bf16[256,640]{1,0:T(8,128)(2,1)S(1)}, u32[]{:S(2)}, u32[]{:S(2)}) collective-permute-start(bf16[256,640]{1,0:T(8,128)(2,1)S(1)} %get-tuple-element.82), channel_id=1, source_target_pairs={{0,4},{1,5},{2,6},{3,7},{4,0},{5,1},{6,2},{7,3},{8,12},{9,13},{10,... | collective-permute-start | bytes 983048 | tf_op jit(solution)/shard_map/ppermute | solution.py:245
  1123.9 30.1 %collective-permute-start.41 = (bf16[256,640]{1,0:T(8,128)(2,1)S(1)}, bf16[256,640]{1,0:T(8,128)(2,1)S(1)}, u32[]{:S(2)}, u32[]{:S(2)}) collective-permute-start(bf16[256,640]{1,0:T(8,128)(2,1)S(1)} %get-tuple-element.83), channel_id=1, source_target_pairs={{0,6},{1,7},{2,0},{3,1},{4,2},{5,3},{6,4},{7,5},{8,14},{9,15},{10,... | collective-permute-start | bytes 983048 | tf_op jit(solution)/shard_map/ppermute | solution.py:245
  1137.1 19.3 %collective-permute-start.33 = (bf16[256,640]{1,0:T(8,128)(2,1)S(1)}, bf16[256,640]{1,0:T(8,128)(2,1)S(1)}, u32[]{:S(2)}, u32[]{:S(2)}) collective-permute-start(bf16[256,640]{1,0:T(8,128)(2,1)S(1)} %fusion.45), channel_id=1, source_target_pairs={{0,8},{8,0},{16,24},{24,16},{1,9},{9,1},{17,25},{25,17},{2,10},{10... | collective-permute-start | bytes 983048 | tf_op jit(solution)/shard_map/ppermute | solution.py:251
  1137.7 20.2 %collective-permute-start.32 = (bf16[256,640]{1,0:T(8,128)(2,1)S(1)}, bf16[256,640]{1,0:T(8,128)(2,1)S(1)}, u32[]{:S(2)}, u32[]{:S(2)}) collective-permute-start(bf16[256,640]{1,0:T(8,128)(2,1)S(1)} %fusion.45), channel_id=1, source_target_pairs={{0,16},{8,24},{16,0},{24,8},{1,17},{9,25},{17,1},{25,9},{2,18},{10... | collective-permute-start | bytes 983048 | tf_op jit(solution)/shard_map/ppermute | solution.py:251
  1140.3 17.5 %collective-permute-start.31 = (bf16[256,640]{1,0:T(8,128)(2,1)S(1)}, bf16[256,640]{1,0:T(8,128)(2,1)S(1)}, u32[]{:S(2)}, u32[]{:S(2)}) collective-permute-start(bf16[256,640]{1,0:T(8,128)(2,1)S(1)} %fusion.45), channel_id=1, source_target_pairs={{0,24},{8,16},{16,8},{24,0},{1,25},{9,17},{17,9},{25,1},{2,26},{10... | collective-permute-start | bytes 983048 | tf_op jit(solution)/shard_map/ppermute | solution.py:251
  1154.3 10.7 collective-permute-start.44
  1154.8 15.3 %collective-permute-start.43 = (bf16[256,640]{1,0:T(8,128)(2,1)S(1)}, bf16[256,640]{1,0:T(8,128)(2,1)S(1)}, u32[]{:S(2)}, u32[]{:S(2)}) collective-permute-start(bf16[256,640]{1,0:T(8,128)(2,1)S(1)} %fusion.42), channel_id=1, source_target_pairs={{0,16},{8,24},{16,0},{24,8},{1,17},{9,25},{17,1},{25,9},{2,18},{10... | collective-permute-start | bytes 983048 | tf_op jit(solution)/shard_map/ppermute | solution.py:251
  1156.4 15.5 %collective-permute-start.42 = (bf16[256,640]{1,0:T(8,128)(2,1)S(1)}, bf16[256,640]{1,0:T(8,128)(2,1)S(1)}, u32[]{:S(2)}, u32[]{:S(2)}) collective-permute-start(bf16[256,640]{1,0:T(8,128)(2,1)S(1)} %fusion.42), channel_id=1, source_target_pairs={{0,24},{8,16},{16,8},{24,0},{1,25},{9,17},{17,9},{25,1},{2,26},{10... | collective-permute-start | bytes 983048 | tf_op jit(solution)/shard_map/ppermute | solution.py:251
  (44 other events, 184.8 us)
